TPU v7x, 32 devices: a whole 2x2x4 slice. The times are simulated.
32 devices in a mesh: dp: 4 (over y, x), seq: 8 (over z, core).
Axes of the slice: x: 2, y: 2, z: 4, core: 2. Of those that a mesh axis runs over, the one named last changes fastest.
Arguments:
- tokens_in: bfloat16 [4, 1024, 12288], P('dp', 'seq'), may hold values from -6 to 6
- short_filter: float32 [7, 12288], replicated, may hold values from -2 to 2
- long_filter: bfloat16 [256, 128], replicated, may hold values from -0.5 to 0.5
- out_weight: bfloat16 [4096, 4096], P('dp', 'seq'), may hold values from -0.09375 to 0.09375
- cotangent: bfloat16 [4, 1024, 4096], P('dp', None, 'seq'), may hold values from -6 to 6
Outputs:
- block_out: bfloat16 [4, 1024, 4096], P('dp', None, 'seq')
- grad_tokens: bfloat16 [4, 1024, 12288], P('dp', 'seq')
- grad_short: float32 [7, 12288], replicated
- grad_long: float32 [256, 128], replicated
- grad_weight: float32 [4096, 4096], P('dp', 'seq')
All inputs are finite; a program needn't handle non-finite values.
Results may differ from a plain program's by a relative error of at most 0.023.
Values may be sent and summed in bfloat16 or wider, within the bound.
A program may use at most 192 MiB of HBM per device.

v0:
```python
import jax
import jax.numpy as jnp
from jax import lax
from jax.sharding import PartitionSpec as P


def shifted(x, axis, by):
    size = lax.axis_size(axis)
    pairs = [(i, i + by) for i in range(size) if 0 <= i + by < size]
    return lax.ppermute(x, axis, pairs)


def tap_table(filters, tap_index):
    tap_count = filters.shape[1]
    valid = (tap_index >= 0) & (tap_index < tap_count)
    clipped = jnp.clip(tap_index, 0, tap_count - 1)
    taken = jnp.take(filters, clipped, axis=1)
    return jnp.where(valid[None], taken, jnp.zeros((), filters.dtype))


def forward_table(filters):
    tap_count = filters.shape[1]
    row_pos = jnp.arange(tap_count, dtype=jnp.int32)[:, None]
    col_pos = jnp.arange(2 * tap_count, dtype=jnp.int32)[None, :]
    return tap_table(filters, row_pos + tap_count - col_pos)


def adjoint_table(filters):
    tap_count = filters.shape[1]
    row_pos = jnp.arange(tap_count, dtype=jnp.int32)[:, None]
    col_pos = jnp.arange(2 * tap_count, dtype=jnp.int32)[None, :]
    return tap_table(filters, col_pos - row_pos)


def windows(padded, row_count, tap_count, group_count):
    channels = padded.shape[1]
    blocks = row_count // tap_count
    leading = padded[:row_count].reshape(blocks, tap_count, group_count, channels // group_count)
    trailing = padded[tap_count : tap_count + row_count].reshape(
        blocks, tap_count, group_count, channels // group_count
    )
    return jnp.concatenate([leading, trailing], axis=1)


def medium_grad(grad_in, window, tap_count, group_count):
    blocks = grad_in.shape[0] // tap_count
    grad_blocks = grad_in.reshape(blocks, tap_count, group_count, -1)
    products = jnp.einsum("bigk,brgk->gir", grad_blocks, window, preferred_element_type=jnp.float32)
    flattened = products.reshape(group_count, tap_count * 2 * tap_count)
    flattened = jnp.concatenate(
        [flattened, jnp.zeros((group_count, tap_count), jnp.float32)], axis=1
    )
    skewed = flattened.reshape(group_count, tap_count, 2 * tap_count + 1)
    summed = jnp.sum(skewed[:, :, 1 : tap_count + 1], axis=1)
    return summed[:, ::-1]


def short_forward(extended, weights, row_count):
    short_taps = weights.shape[0]
    accumulated = jnp.zeros((row_count, extended.shape[1]), jnp.float32)
    for tap_index in range(short_taps):
        start_row = short_taps - 1 - tap_index
        accumulated = accumulated + weights[tap_index] * extended[
            start_row : start_row + row_count
        ].astype(jnp.float32)
    return accumulated


def short_adjoint(extended, weights, row_count):
    short_taps = weights.shape[0]
    accumulated = jnp.zeros((row_count, extended.shape[1]), jnp.float32)
    for tap_index in range(short_taps):
        accumulated = accumulated + weights[tap_index] * extended[
            tap_index : tap_index + row_count
        ].astype(jnp.float32)
    return accumulated


def short_grad(grads, extended, row_count):
    short_taps = extended.shape[0] - row_count + 1
    grads_wide = grads.astype(jnp.float32)
    pieces_list = []
    for tap_index in range(short_taps):
        start_row = short_taps - 1 - tap_index
        pieces_list.append(
            jnp.sum(
                grads_wide * extended[start_row : start_row + row_count].astype(jnp.float32), axis=0
            )
        )
    return jnp.stack(pieces_list, axis=0)


def shards(tokens_in, short_filter, long_filter, out_weight, cotangent):
    tokens = tokens_in[0]
    row_count = tokens.shape[0]
    channels = tokens.shape[1] // 3
    short_taps = short_filter.shape[0]
    tap_count = long_filter.shape[1]
    group_count = long_filter.shape[0]
    lead_rim = shifted(tokens[row_count - (short_taps - 1) :], "seq", 1)
    u_ext = jnp.concatenate([lead_rim, tokens], axis=0)
    features = short_forward(u_ext, short_filter, row_count)
    query_part = features[:, :channels]
    key_part = features[:, channels : 2 * channels]
    value_part = features[:, 2 * channels :]
    mixer_in = (key_part * value_part).astype(jnp.bfloat16)
    mixer_lead = shifted(mixer_in[row_count - (tap_count - 1) :], "seq", 1)
    padded = jnp.concatenate([jnp.zeros((1, channels), jnp.bfloat16), mixer_lead, mixer_in], axis=0)
    window = windows(padded, row_count, tap_count, group_count)
    mixed = jnp.einsum(
        "gir,brgk->bigk", forward_table(long_filter), window, preferred_element_type=jnp.float32
    )
    mixed = mixed.reshape(row_count, channels)
    gated = (query_part * mixed).astype(jnp.bfloat16)
    weights = lax.all_gather(out_weight, "dp", axis=0, tiled=True)
    upstream = cotangent[0]
    all_rows = lax.all_gather(gated, "seq", axis=0, tiled=True)
    output = jnp.dot(all_rows, weights, preferred_element_type=jnp.float32)
    weight_grad = lax.dot_general(
        all_rows, upstream, (((0,), (0,)), ((), ())), preferred_element_type=jnp.float32
    )
    grad_weight = lax.psum_scatter(
        weight_grad.astype(jnp.bfloat16), "dp", scatter_dimension=0, tiled=True
    ).astype(jnp.float32)
    grad_gated = lax.psum_scatter(
        lax.dot_general(
            upstream, weights, (((1,), (1,)), ((), ())), preferred_element_type=jnp.float32
        ).astype(jnp.bfloat16),
        "seq",
        scatter_dimension=0,
        tiled=True,
    ).astype(jnp.float32)
    grad_mixed_in = (grad_gated * query_part).astype(jnp.bfloat16)
    grad_next = shifted(grad_mixed_in[: tap_count - 1], "seq", -1)
    grad_pad = jnp.concatenate(
        [grad_mixed_in, grad_next, jnp.zeros((1, channels), jnp.bfloat16)], axis=0
    )
    grad_window = windows(grad_pad, row_count, tap_count, group_count)
    grad_mixer = jnp.einsum(
        "gpq,bqgk->bpgk",
        adjoint_table(long_filter),
        grad_window,
        preferred_element_type=jnp.float32,
    )
    grad_mixer = grad_mixer.reshape(row_count, channels)
    grad_features = jnp.concatenate(
        [grad_gated * mixed, grad_mixer * value_part, grad_mixer * key_part], axis=1
    ).astype(jnp.bfloat16)
    long_local = medium_grad(grad_mixed_in, window, tap_count, group_count)
    grad_long = lax.psum(long_local, ("dp", "seq"))
    feature_next = shifted(grad_features[: short_taps - 1], "seq", -1)
    grad_ext = jnp.concatenate([grad_features, feature_next], axis=0)
    grad_tokens = short_adjoint(grad_ext, short_filter, row_count).astype(jnp.bfloat16)
    short_local = short_grad(grad_features, u_ext, row_count)
    grad_short = lax.psum(short_local, ("dp", "seq"))
    return (
        output.astype(jnp.bfloat16)[None],
        grad_tokens[None],
        grad_short,
        grad_long,
        grad_weight,
    )


def solution(mesh):
    return jax.shard_map(
        shards,
        mesh=mesh,
        in_specs=(P("dp", "seq", None), P(), P(), P("dp", "seq"), P("dp", None, "seq")),
        out_specs=(P("dp", None, "seq"), P("dp", "seq", None), P(), P(), P("dp", "seq")),
        check_vma=False,
    )
```

profile of v0, /device:TPU:0, one launch (start us, length us, event | category | flops | bytes accessed | tf_op | source)
XLA Modules:
  0.0 864.1 jit_solution(9280638382427493510)
XLA Ops:
  8.0 57.3 %all-gather.5.cloned.1.call-done = bf16[4096,512]{1,0:T(8,128)(2,1)} async-done(((bf16[1024,512]{1,0:T(8,128)(2,1)}), bf16[4096,512]{1,0:T(8,128)(2,1)}) %all-gather.5.cloned.1.call-update) | async-done | bytes 4194320 | tf_op jit(solution)/shard_map/all_gather | solution.py:115
  65.3 8.9 %convolution_convert_fusion = bf16[1024,4096]{1,0:T(8,128)(2,1)} fusion(bf16[4096,512]{1,0:T(8,128)(2,1)} %all-gather.5.cloned.1.call-done, bf16[1,1024,512]{2,1,0:T(8,128)(2,1)S(1)} %copy-done), kind=kOutput, calls=%fused_computation.37 | convolution fusion | flops 4299161600 | bytes 13631488 | tf_op jit(solution)/shard_map/dot_general | solution.py:126
  78.8 14.5 %fusion.17 = f32[128,12288]{1,0:T(8,128)} fusion(bf16[128,12288]{1,0:T(8,128)(2,1)} %bitcast.75, bf16[6,12288]{1,0:T(8,128)(2,1)S(1)} %collective-permute-done, f32[12288]{0:T(1024)S(1)} %bitcast.99, f32[12288]{0:T(1024)S(1)} %bitcast.101, f32[12288]{0:T(1024)S(1)} %bitcast.91, f32[12288]{0:T(1024)S(1)} %bitcast.93, f32[12288]{0:T(1024)S(1)} %bitcast.95, ...), kind=kLoop, calls=%fused_computation.43 | loop fusion | flops 59768832 | bytes 9928704 | tf_op jit(solution)/shard_map/add | solution.py:63
  93.3 70.7 %reduce-scatter.3.cloned.1.call-done = bf16[128,4096]{1,0:T(8,128)(2,1)} async-done(((bf16[1024,4096]{1,0:T(8,128)(2,1)}), bf16[128,4096]{1,0:T(8,128)(2,1)}) %reduce-scatter.3.cloned.1.call-update) | async-done | bytes 1048592 | tf_op jit(solution)/shard_map/reduce_scatter | solution.py:125
  164.0 2.1 fusion.39
  167.8 129.4 %gather_fusion.1 = bf16[32768,256]{1,0:T(8,128)(2,1)} fusion(bf16[256,128]{0,1:T(8,128)(2,1)S(1)} %copy.38, s32[32768]{0:T(1024)S(1)} %broadcast_clamp_fusion), kind=kCustom, calls=%fused_computation.1.clone | custom fusion | bytes 33685504 | tf_op jit(solution)/shard_map/jit(_take)/gather | solution.py:17
  297.2 23.1 %copy.45 = bf16[128,256,256]{1,0,2:T(8,128)(2,1)} copy(bf16[128,256,256]{2,1,0:T(8,128)(2,1)} %bitcast.74) | data formatting | bytes 33554432 | tf_op jit(solution)/shard_map/jit(_take)/gather | solution.py:17
  324.2 11.9 %fusion = f32[256,16,128]{2,1,0:T(8,128)} fusion(bf16[128,256,256]{1,0,2:T(8,128)(2,1)} %copy.45, pred[128,256]{1,0:T(8,128)(4,1)S(1)} %get-tuple-element.38, pred[128,256]{1,0:T(8,128)(4,1)S(1)} %get-tuple-element.39, bf16[1,128,256,16]{1,3,2,0:T(8,128)(2,1)} %bitcast.86, bf16[1,128,256,16]{1,3,2,0:T(8,128)(2,1)S(1)} %bitcast.79), kind=kOutput, calls=%fused_computation.12 | convolution fusion | flops 289406976 | bytes 21037056 | tf_op jit(solution)/shard_map/gpq,bqgk->bpgk/dot_general | solution.py:139
  336.1 2.9 copy.46
  339.0 3.4 multiply_convert_fusion.1
  344.7 16.1 %collective-permute-start.1 = (bf16[127,4096]{1,0:T(8,128)(2,1)}, bf16[127,4096]{1,0:T(8,128)(2,1)}, u32[]{:S(2)}, u32[]{:S(2)}) collective-permute-start(bf16[127,4096]{1,0:T(8,128)(2,1)} %slice.142), channel_id=1, source_target_pairs={{0,1},{1,2},{2,3},{3,4},{4,5},{5,6},{6,7},{8,9},{9,10},{10,11},{11... | collective-permute-start | bytes 3121160 | tf_op jit(solution)/shard_map/ppermute | solution.py:10
  360.9 129.4 %gather_fusion = bf16[32768,256]{1,0:T(8,128)(2,1)} fusion(bf16[256,128]{0,1:T(8,128)(2,1)S(1)} %copy.38, s32[32768]{0:T(1024)S(1)} %broadcast_clamp_fusion.1), kind=kCustom, calls=%fused_computation.clone | custom fusion | bytes 33685504 | tf_op jit(solution)/shard_map/jit(_take)/gather | solution.py:17
  490.2 22.9 %copy.39 = bf16[128,256,256]{1,0,2:T(8,128)(2,1)} copy(bf16[128,256,256]{2,1,0:T(8,128)(2,1)} %bitcast.73) | data formatting | bytes 33554432 | tf_op jit(solution)/shard_map/jit(_take)/gather | solution.py:17
  513.3 2.3 copy.37
  515.6 2.3 copy.52
  517.9 2.6 concatenate.26.clone
  520.5 12.2 %fusion.1 = f32[256,16,128]{2,1,0:T(8,128)} fusion(bf16[128,256,256]{1,0,2:T(8,128)(2,1)} %copy.39, pred[128,256]{1,0:T(8,128)(4,1)S(1)} %get-tuple-element.37, pred[128,256]{1,0:T(8,128)(4,1)S(1)} %get-tuple-element.36, bf16[1,128,256,16]{1,3,2,0:T(8,128)(2,1)} %bitcast.81, bf16[1,128,256,16]{1,3,2,0:T(8,128)(2,1)} %bitcast.77), kind=kOutput, calls=%fused_computation.14 | convolution fusion | flops 289406976 | bytes 21037056 | tf_op jit(solution)/shard_map/gir,brgk->bigk/dot_general | solution.py:110
  532.7 2.9 copy.40
  535.6 4.3 fusion.38
  540.0 18.4 %fusion.43 = f32[256,128,256]{2,1,0:T(8,128)} fusion(bf16[128,256,16]{0,2,1:T(8,128)(2,1)} %bitcast.80, bf16[1,128,256,16]{1,3,2,0:T(8,128)(2,1)} %bitcast.82, bf16[1,128,256,16]{1,3,2,0:T(8,128)(2,1)} %bitcast.78), kind=kOutput, calls=%fused_computation.82 | convolution fusion | flops 272629760 | bytes 36700160 | tf_op jit(solution)/shard_map/bigk,brgk->gir/dot_general | solution.py:48
  558.4 35.1 %copy.51 = f32[256,128,256]{0,2,1:T(8,128)} copy(f32[256,128,256]{2,1,0:T(8,128)} %fusion.43) | data formatting | bytes 67108864 | tf_op jit(solution)/shard_map/reshape | solution.py:49
  593.5 22.6 %concatenate.32 = f32[256,32896]{0,1:T(8,128)} pad(f32[256,32768]{0,1:T(8,128)} %bitcast.72, f32[]{:T(128)} %constant.2.clone.1), padding=0_0x0_128 | pad | bytes 67239936 | tf_op jit(solution)/shard_map/concatenate | solution.py:50
  616.1 28.5 %reshape.106 = f32[256,128,257]{0,2,1:T(8,128)} reshape(f32[256,32896]{0,1:T(8,128)} %concatenate.32) | data formatting | bytes 67371008 | tf_op jit(solution)/shard_map/reshape | solution.py:53
  644.6 8.2 slice_reduce_fusion
  653.5 15.7 %fusion.30 = (f32[12288]{0:T(1024)S(1)}, f32[12288]{0:T(1024)S(1)}, f32[12288]{0:T(1024)S(1)}, f32[12288]{0:T(1024)S(1)}, f32[12288]{0:T(1024)}, /*index=5*/f32[12288]{0:T(1024)}, f32[12288]{0:T(1024)}) fusion(bf16[128,12288]{1,0:T(8,128)(2,1)} %bitcast.76, bf16[6,12288]{1,0:T(8,128)(2,1)S(1)} %copy-done.5, bf16[128,4096]{1,0:T(8,128)(2,1)S(1)} %get-tuple-element.21, ...), kind=kLoop, calls=%fused_computation.56 | loop fusion | flops 70692864 | bytes 9928704 | tf_op jit(solution)/shard_map/reduce_sum | solution.py:86
  671.3 9.7 %convolution_convert_fusion.1 = bf16[4096,512]{1,0:T(8,128)(2,1)} fusion(bf16[1024,4096]{1,0:T(8,128)(2,1)} %all-gather.3.cloned.1.call-done, bf16[1,1024,512]{2,1,0:T(8,128)(2,1)S(1)} %copy-done), kind=kOutput, calls=%fused_computation.58 | convolution fusion | flops 4297064448 | bytes 13631488 | tf_op jit(solution)/shard_map/dot_general | solution.py:119
  686.0 2.2 pad_maximum_fusion
  688.4 8.1 fusion.37
  696.4 102.4 %all-reduce.6.cloned.1.call-done = (f32[7,12288]{1,0:T(8,128)}, f32[256,128]{0,1:T(8,128)}) async-done(((f32[7,12288]{1,0:T(8,128)}, f32[256,128]{0,1:T(8,128)}), (f32[7,12288]{1,0:T(8,128)}, f32[256,128]{0,1:T(8,128)})) %all-reduce.6.cloned.1.call-update) | async-done | bytes 475152 | tf_op jit(solution)/shard_map/psum | solution.py:155
  800.5 10.1 %fusion.42 = bf16[1,1024,512]{2,1,0:T(8,128)(2,1)} fusion(bf16[1024,4096]{1,0:T(8,128)(2,1)} %all-gather.3.cloned.1.call-done, bf16[4096,512]{1,0:T(8,128)(2,1)} %all-gather.5.cloned.1.call-done), kind=kOutput, calls=%fused_computation.81 | convolution fusion | flops 4295491584 | bytes 13631488 | tf_op jit(solution)/shard_map/dot_general | solution.py:118
  810.6 43.1 %reduce-scatter.5.cloned.1.call-done = bf16[1024,512]{1,0:T(8,128)(2,1)} async-done(((bf16[4096,512]{1,0:T(8,128)(2,1)}), bf16[1024,512]{1,0:T(8,128)(2,1)}) %reduce-scatter.5.cloned.1.call-update) | async-done | bytes 1048592 | tf_op jit(solution)/shard_map/reduce_scatter | solution.py:122
  853.7 2.8 convert_element_type.100
  (86 shorter events, 23.3 us)
Async XLA Ops:
  7.2 58.1 %copy-start = (bf16[1,1024,512]{2,1,0:T(8,128)(2,1)S(1)}, bf16[1,1024,512]{2,1,0:T(8,128)(2,1)}, u32[]{:S(2)}) copy-start(bf16[1,1024,512]{2,1,0:T(8,128)(2,1)} %param.11) | copy-start | bytes 3145732
  7.2 58.1 %all-gather.5.cloned.1.call-start = ((), (), s32[]{:S(2)}) async-start(), calls=%async_computation.3 | async-start | bytes 5242880 | tf_op jit(solution)/shard_map/all_gather | solution.py:115
  7.9 156.1 %reduce-scatter.3.cloned.1.call-start = ((), (), s32[]{:S(2)}) async-start(), calls=%async_computation.4 | async-start | bytes 9437184 | tf_op jit(solution)/shard_map/reduce_scatter | solution.py:125
  74.2 2.9 copy-start.21
  74.2 597.0 %all-gather.3.cloned.1.call-start = ((), (), s32[]{:S(2)}) async-start(), calls=%async_computation.2 | async-start | bytes 9437184 | tf_op jit(solution)/shard_map/all_gather | solution.py:117
  75.3 2.8 collective-permute-start
  77.3 0.8 copy-start.6
  77.3 0.8 copy-start.8
  77.3 0.8 copy-start.10
  77.4 0.8 copy-start.12
  77.4 0.8 copy-start.14
  77.4 0.8 copy-start.16
  77.4 0.8 copy-start.18
  78.1 0.7 copy-start.4
  78.8 88.7 %copy-start.22 = (bf16[256,128]{1,0:T(8,128)(2,1)S(1)}, bf16[256,128]{1,0:T(8,128)(2,1)}, u32[]{:S(2)}) copy-start(bf16[256,128]{1,0:T(8,128)(2,1)} %param.9) | copy-start | bytes 196612
  166.1 154.9 %collective-permute-start.2 = (bf16[127,4096]{1,0:T(8,128)(2,1)S(1)}, bf16[127,4096]{1,0:T(8,128)(2,1)}, u32[]{:S(2)}, u32[]{:S(2)}) collective-permute-start(bf16[127,4096]{1,0:T(8,128)(2,1)S(1)} %bitcast.83), channel_id=1, source_target_pairs={{1,0},{2,1},{3,2},{4,3},{5,4},{6,5},{7,6},{9,8},{10,9},{11,10},{12... | collective-permute-start | bytes 3121160 | tf_op jit(solution)/shard_map/ppermute | solution.py:10
  321.0 15.1 %copy-start.3 = (bf16[128,4096]{0,1:T(8,128)(2,1)}, bf16[128,4096]{0,1:T(8,128)(2,1)S(1)}, u32[]{:S(2)}) copy-start(bf16[128,4096]{0,1:T(8,128)(2,1)S(1)} %copy.42) | copy-start | bytes 3145732
  342.5 1.0 copy-start.2
  344.7 170.9 %collective-permute-start.1 = (bf16[127,4096]{1,0:T(8,128)(2,1)}, bf16[127,4096]{1,0:T(8,128)(2,1)}, u32[]{:S(2)}, u32[]{:S(2)}) collective-permute-start(bf16[127,4096]{1,0:T(8,128)(2,1)} %slice.142), channel_id=1, source_target_pairs={{0,1},{1,2},{2,3},{3,4},{4,5},{5,6},{6,7},{8,9},{9,10},{10,11},{11... | collective-permute-start | bytes 3121160 | tf_op jit(solution)/shard_map/ppermute | solution.py:10
  540.0 258.9 %all-reduce.6.cloned.1.call-start = ((), (), s32[]{:S(2)}) async-start(), calls=%async_computation.6 | async-start | bytes 1048576 | tf_op jit(solution)/shard_map/psum | solution.py:155
  644.6 8.9 %copy-start.5 = (bf16[6,12288]{1,0:T(8,128)(2,1)S(1)}, bf16[6,12288]{1,0:T(8,128)(2,1)}, u32[]{:S(2)}) copy-start(bf16[6,12288]{1,0:T(8,128)(2,1)} %copy-done.4) | copy-start | bytes 442372
  671.2 182.5 %reduce-scatter.5.cloned.1.call-start = ((), (), s32[]{:S(2)}) async-start(), calls=%async_computation.5 | async-start | bytes 5242880 | tf_op jit(solution)/shard_map/reduce_scatter | solution.py:122
  681.0 5.0 copy-start.1
  681.0 7.3 copy-start.7
  681.0 7.3 copy-start.9
  681.0 7.3 copy-start.11
  681.0 7.3 copy-start.13
  681.1 7.3 copy-start.15
  681.1 7.3 copy-start.17
  681.1 7.3 copy-start.19
  682.5 3.5 collective-permute-start.3
  800.5 56.0 %copy-start.20 = (f32[7,12288]{1,0:T(8,128)S(1)}, f32[7,12288]{1,0:T(8,128)}, u32[]{:S(2)}) copy-start(f32[7,12288]{1,0:T(8,128)} %get-tuple-element.42) | copy-start | bytes 1032196
Sparse Core Ops, SparseCore 0:
  9.9 55.3 all-gather.4
  74.3 89.5 reduce-scatter.2
  540.1 80.6 all-gather.2
  671.3 127.4 all-reduce.5
  801.9 51.6 reduce-scatter.4
where the time goes:
time: 869 us; the launch traced here: 864 us
  local copies, waits for them, and re-layouts  417 us (48%)
  waiting for transfers between devices  277 us (32%)
  matrix products  71.3 us (8%)
  other arithmetic  63.3 us (7%)
  starting transfers between devices  20.9 us (2%)
  between operations  14.6 us (2%)
    gather x4, local copies, waits for them, and re-layouts, tap_table(): taken = jnp.take(filters, clipped, axis=1)  305 us
    psum x1, waiting for transfers between devices, shards(): grad_short = lax.psum(short_local, ('dp', 'seq'))  102 us
    reduce_scatter x1, waiting for transfers between devices, shards(): lax.psum_scatter(lax.dot_general(upstream, weights, (((1,), (1,)), ((), (...  70.7 us
    all_gather x1, waiting for transfers between devices, shards(): weights = lax.all_gather(out_weight, 'dp', axis=0, tiled=True)  57.3 us
    reduce_scatter x1, waiting for transfers between devices, shards(): lax.psum_scatter(weight_grad.astype(jnp.bfloat16), 'dp', scatter_dimensio...  43.1 us
    reshape x1, local copies, waits for them, and re-layouts, medium_grad(): flattened = products.reshape(group_count, tap_count * 2 * tap_count)  35.1 us
    reshape x1, local copies, waits for them, and re-layouts, medium_grad(): skewed = flattened.reshape(group_count, tap_count, 2 * tap_count + 1)  28.5 us
    concatenate x1, local copies, waits for them, and re-layouts, medium_grad(): jnp.concatenate([flattened, jnp.zeros((group_count, tap_count), jnp.float...  22.6 us
  transfers between devices with their start and end apart: 9, of which 6 were waited for; matrix products, arithmetic and copies ran while one was open for 57% of the time, Pallas kernels for 0%

commit v1 on v0

v1 whole, which is shorter than its diff:
```python
import functools

import jax
import jax.numpy as jnp
from jax import lax
from jax.experimental import pallas as pl
from jax.experimental.pallas import tpu as pltpu
from jax.sharding import PartitionSpec as P

LANES = 128
HALO = 8
BF = jnp.bfloat16
F32 = jnp.float32


def shifted(x, axis, by):
    size = lax.axis_size(axis)
    pairs = [(i, i + by) for i in range(size) if 0 <= i + by < size]
    return lax.ppermute(x, axis, pairs)


def features_kernel(tok_ref, rim_ref, w_ref, feat_ref, mix_ref, ext, key):
    part = pl.program_id(1)
    rows, width = tok_ref.shape
    taps = w_ref.shape[0]

    def lane_block(b, carry):
        sl = pl.ds(pl.multiple_of(b * LANES, LANES), LANES)
        ext[0:HALO, :] = rim_ref[:, sl]
        ext[HALO : HALO + rows, :] = tok_ref[:, sl].astype(F32)
        w = w_ref[:, sl]
        acc = jnp.zeros((rows, LANES), F32)
        for j in range(taps):
            acc = acc + w[j : j + 1] * ext[HALO - j : HALO - j + rows, :]
        feat_ref[:, sl] = acc

        @pl.when(part == 1)
        def _():
            key[:, sl] = acc

        @pl.when(part == 2)
        def _():
            mix_ref[:, sl] = (acc * key[:, sl]).astype(BF)

        return carry

    lax.fori_loop(0, width // LANES, lane_block, 0)


def group_tables(filt_ref, b, per, table, lower_first):
    taps = filt_ref.shape[1]
    row = lax.broadcasted_iota(jnp.int32, (taps, taps), 0)
    col = lax.broadcasted_iota(jnp.int32, (taps, taps), 1)
    first = (col >= row) if lower_first else (col > row)
    filt = filt_ref[pl.ds(pl.multiple_of(b * per, per), per), :]
    for g in range(per):
        base = jnp.broadcast_to(filt[g : g + 1, :], (taps, taps))
        circ = pltpu.roll(base, 0, 1, stride=1, stride_axis=0)
        table[g * taps : (g + 1) * taps, 0:taps] = jnp.where(first, circ, 0.0).astype(BF)
        table[g * taps : (g + 1) * taps, taps : 2 * taps] = jnp.where(first, 0.0, circ).astype(BF)


def pick_groups(stacked, per, rows):
    size = LANES // per
    lane = lax.broadcasted_iota(jnp.int32, (rows, LANES), 1)
    out = stacked[0:rows]
    for g in range(1, per):
        out = jnp.where(lane >= g * size, stacked[g * rows : (g + 1) * rows], out)
    return out


def mixed_kernel(per, mix_ref, lead_ref, query_ref, filt_ref, mixed_ref, gated_ref, table, win):
    rows, width = mix_ref.shape

    def lane_block(b, carry):
        sl = pl.ds(pl.multiple_of(b * LANES, LANES), LANES)
        group_tables(filt_ref, b, per, table, False)
        win[0:rows, :] = lead_ref[:, sl]
        win[rows : 2 * rows, :] = mix_ref[:, sl]
        stacked = jnp.dot(table[...], win[...], preferred_element_type=F32)
        mixed = pick_groups(stacked, per, rows)
        mixed_ref[:, sl] = mixed
        gated_ref[:, sl] = (query_ref[:, sl] * mixed).astype(BF)
        return carry

    lax.fori_loop(0, width // LANES, lane_block, 0)


def backward_kernel(
    per, gg_ref, next_ref, query_ref, key_ref, value_ref, mixed_ref, mix_ref, lead_ref,
    filt_ref, tok_ref, rim_ref, w_ref,
    gtok_ref, tail_ref, head_ref, gshort_ref, glong_ref,
    table, win, masked, gf, ext,
):
    part = pl.program_id(1)
    rows, width = gg_ref.shape
    taps = w_ref.shape[0]
    size = LANES // per
    blocks = width // LANES

    @pl.when(part == 0)
    def _():
        row = lax.broadcasted_iota(jnp.int32, (rows, rows), 0)
        col = lax.broadcasted_iota(jnp.int32, (rows, rows), 1)
        flip = jnp.where(row + col == rows - 1, 1.0, 0.0).astype(BF)
        lead_side = col + row > rows - 1
        lane = lax.broadcasted_iota(jnp.int32, (rows, LANES), 1)

        def lane_block(b, carry):
            sl = pl.ds(pl.multiple_of(b * LANES, LANES), LANES)
            gg = gg_ref[:, sl].astype(F32)
            gm = (gg * query_ref[:, sl]).astype(BF)
            group_tables(filt_ref, b, per, table, True)
            win[0:rows, :] = gm
            win[rows : 2 * rows, :] = next_ref[:, sl]
            stacked = jnp.dot(table[...], win[...], preferred_element_type=F32)
            gmix = pick_groups(stacked, per, rows)
            parts = (gg * mixed_ref[:, sl], gmix * value_ref[:, sl], gmix * key_ref[:, sl])
            for p in range(3):
                gf[p, 0:rows, sl] = parts[p].astype(BF).astype(F32)
                gf[p, rows : rows + HALO, sl] = jnp.zeros((HALO, LANES), F32)
            rev = jnp.dot(flip, gm, preferred_element_type=F32)
            for g in range(per):
                mine = (lane >= g * size) & (lane < (g + 1) * size)
                masked[g * rows : (g + 1) * rows, :] = jnp.where(mine, rev, 0.0).astype(BF)
            win[0:rows, :] = lead_ref[:, sl]
            win[rows : 2 * rows, :] = mix_ref[:, sl]
            prods = lax.dot_general(
                masked[...], win[...], (((1,), (1,)), ((), ())), preferred_element_type=F32
            )
            sums = []
            for g in range(per):
                one = prods[g * rows : (g + 1) * rows]
                fold = jnp.where(lead_side, one[:, 0:rows], one[:, rows : 2 * rows])
                turned = pltpu.roll(fold, 0, 1, stride=1, stride_axis=0)
                sums.append(jnp.sum(turned, axis=0, keepdims=True))
            glong_ref[pl.ds(pl.multiple_of(b * per, per), per), :] = jnp.concatenate(sums, axis=0)
            return carry

        lax.fori_loop(0, blocks, lane_block, 0)

    def short_block(b, carry):
        sl = pl.ds(pl.multiple_of(b * LANES, LANES), LANES)
        ext[0:HALO, :] = rim_ref[:, sl]
        ext[HALO : HALO + rows, :] = tok_ref[:, sl].astype(F32)
        w = w_ref[:, sl]
        own = gf[part, 0:rows, sl]
        head_ref[:, sl] = own[0:HALO]
        acc = w[0:1] * own
        sums = [jnp.sum(own * ext[HALO : HALO + rows, :], axis=0, keepdims=True)]
        for j in range(1, taps):
            acc = acc + w[j : j + 1] * gf[part, j : j + rows, sl]
            sums.append(
                jnp.sum(own * ext[HALO - j : HALO - j + rows, :], axis=0, keepdims=True)
            )
        for _ in range(HALO - taps):
            sums.append(jnp.zeros((1, LANES), F32))
        gtok_ref[:, sl] = acc.astype(BF)
        tail_ref[:, sl] = acc[rows - HALO : rows]
        gshort_ref[:, sl] = jnp.concatenate(sums, axis=0)
        return carry

    lax.fori_loop(0, blocks, short_block, 0)


def reduce_kernel(n_dp, n_seq, x_ref, y_ref, got_dp, half, got_seq, full, s1, r1, s2, r2, s3, r3, s4, r4):
    dp = lax.axis_index("dp")
    seq = lax.axis_index("seq")
    mesh_id = pl.DeviceIdType.MESH

    def dp_peer(k):
        return (lax.rem(dp + k, n_dp), seq)

    def seq_peer(k):
        return (dp, lax.rem(seq + k, n_seq))

    barrier = pltpu.get_barrier_semaphore()
    for k in range(1, n_dp):
        pl.semaphore_signal(barrier, inc=1, device_id=dp_peer(k), device_id_type=mesh_id)
    for k in range(1, n_seq):
        pl.semaphore_signal(barrier, inc=1, device_id=seq_peer(k), device_id_type=mesh_id)
    pl.semaphore_wait(barrier, n_dp + n_seq - 2)

    def exchange(count, peer, source, target, send, recv):
        copies = []
        for k in range(1, count):
            copy = pltpu.make_async_remote_copy(
                src_ref=source(k), dst_ref=target(k), send_sem=send.at[k - 1],
                recv_sem=recv.at[k - 1], device_id=peer(k), device_id_type=mesh_id,
            )
            copy.start()
            copies.append(copy)
        for copy in copies:
            copy.wait()

    exchange(n_dp, dp_peer, lambda k: x_ref.at[lax.rem(dp + k, n_dp)],
             lambda k: got_dp.at[k - 1], s1, r1)
    total = x_ref[dp]
    for k in range(1, n_dp):
        total = total + got_dp[k - 1]
    half[...] = total
    exchange(n_seq, seq_peer, lambda k: half.at[lax.rem(seq + k, n_seq)],
             lambda k: got_seq.at[k - 1], s2, r2)
    total = half[seq]
    for k in range(1, n_seq):
        total = total + got_seq[k - 1]
    full[dp, seq] = total
    exchange(n_seq, seq_peer, lambda k: full.at[dp, seq], lambda k: full.at[dp, seq], s3, r3)
    exchange(n_dp, dp_peer, lambda k: full.at[dp], lambda k: full.at[dp], s4, r4)
    y_ref[...] = full[...]


def all_reduce_small(flat):
    n_dp, n_seq = lax.axis_size("dp"), lax.axis_size("seq")
    devices = n_dp * n_seq
    size = flat.shape[0]
    per = -(-size // (devices * 8 * LANES)) * 8
    padded = jnp.pad(flat, (0, devices * per * LANES - size))
    x = padded.reshape(n_dp, n_seq, per, LANES)
    dma = pltpu.SemaphoreType.DMA
    out = pl.pallas_call(
        functools.partial(reduce_kernel, n_dp, n_seq),
        out_shape=jax.ShapeDtypeStruct(x.shape, F32),
        in_specs=[pl.BlockSpec(memory_space=pltpu.VMEM)],
        out_specs=pl.BlockSpec(memory_space=pltpu.VMEM),
        scratch_shapes=[
            pltpu.VMEM((n_dp - 1, n_seq, per, LANES), F32),
            pltpu.VMEM((n_seq, per, LANES), F32),
            pltpu.VMEM((n_seq - 1, per, LANES), F32),
            pltpu.VMEM(x.shape, F32),
            dma((n_dp - 1,)), dma((n_dp - 1,)),
            dma((n_seq - 1,)), dma((n_seq - 1,)),
            dma((n_seq - 1,)), dma((n_seq - 1,)),
            dma((n_dp - 1,)), dma((n_dp - 1,)),
        ],
        compiler_params=pltpu.CompilerParams(
            collective_id=0, has_side_effects=True, vmem_limit_bytes=16 << 20
        ),
        cost_estimate=pl.CostEstimate(flops=size, bytes_accessed=8 * size, transcendentals=0),
    )(x)
    return out.reshape(-1)[:size]


def shards(tokens_in, short_filter, long_filter, out_weight, cotangent):
    tokens = tokens_in[0]
    row_count = tokens.shape[0]
    channels = tokens.shape[1] // 3
    short_taps = short_filter.shape[0]
    group_count, tap_count = long_filter.shape
    per = LANES * group_count // channels
    width = min(1024, channels)
    nb = channels // width
    groups = group_count // nb
    limit = 40 << 20

    weights = lax.all_gather(out_weight, "dp", axis=0, tiled=True)
    upstream = cotangent[0]
    rim = shifted(tokens[row_count - HALO :], "seq", 1).astype(F32)
    filt = long_filter.astype(F32)
    turned = jnp.roll(filt[:, ::-1], 1, axis=1)

    by_part = lambda rows: pl.BlockSpec((rows, width), lambda j, p: (0, p * nb + j))
    features, mixer_in = pl.pallas_call(
        features_kernel,
        grid=(nb, 3),
        in_specs=[by_part(row_count), by_part(HALO), by_part(short_taps)],
        out_specs=[by_part(row_count), pl.BlockSpec((row_count, width), lambda j, p: (0, j))],
        out_shape=[
            jax.ShapeDtypeStruct((row_count, 3 * channels), F32),
            jax.ShapeDtypeStruct((row_count, channels), BF),
        ],
        scratch_shapes=[
            pltpu.VMEM((row_count + HALO, LANES), F32),
            pltpu.VMEM((row_count, width), F32),
        ],
        compiler_params=pltpu.CompilerParams(vmem_limit_bytes=limit),
        cost_estimate=pl.CostEstimate(
            flops=42 * row_count * channels, bytes_accessed=20 * row_count * channels, transcendentals=0
        ),
    )(tokens, rim, short_filter)
    lead = shifted(mixer_in, "seq", 1)

    col = lambda off: pl.BlockSpec((row_count, width), lambda j: (0, off * nb + j))
    mixed, gated = pl.pallas_call(
        functools.partial(mixed_kernel, per),
        grid=(nb,),
        in_specs=[col(0), col(0), col(0), pl.BlockSpec((groups, tap_count), lambda j: (j, 0))],
        out_specs=[col(0), col(0)],
        out_shape=[
            jax.ShapeDtypeStruct((row_count, channels), F32),
            jax.ShapeDtypeStruct((row_count, channels), BF),
        ],
        scratch_shapes=[
            pltpu.VMEM((per * tap_count, 2 * tap_count), BF),
            pltpu.VMEM((2 * tap_count, LANES), BF),
        ],
        compiler_params=pltpu.CompilerParams(vmem_limit_bytes=limit),
        cost_estimate=pl.CostEstimate(
            flops=4 * per * tap_count * row_count * channels,
            bytes_accessed=14 * row_count * channels, transcendentals=0,
        ),
    )(mixer_in, lead, features, turned)

    all_rows = lax.all_gather(gated, "seq", axis=0, tiled=True)
    grad_gated = lax.psum_scatter(
        lax.dot_general(
            upstream, weights, (((1,), (1,)), ((), ())), preferred_element_type=F32
        ).astype(BF),
        "seq",
        scatter_dimension=0,
        tiled=True,
    )
    weight_grad = lax.dot_general(
        all_rows, upstream, (((0,), (0,)), ((), ())), preferred_element_type=F32
    )
    grad_weight = lax.psum_scatter(
        weight_grad.astype(BF), "dp", scatter_dimension=0, tiled=True
    ).astype(F32)
    output = jnp.dot(all_rows, weights, preferred_element_type=F32).astype(BF)

    grad_mixed_in = (grad_gated.astype(F32) * features[:, :channels]).astype(BF)
    grad_next = shifted(grad_mixed_in, "seq", -1)
    at = lambda off: pl.BlockSpec((row_count, width), lambda j, p: (0, off * nb + j))
    group_spec = pl.BlockSpec((groups, tap_count), lambda j, p: (j, 0))
    grad_tokens, tail, head, short_local, long_local = pl.pallas_call(
        functools.partial(backward_kernel, per),
        grid=(nb, 3),
        in_specs=[
            at(0), at(0), at(0), at(1), at(2), at(0), at(0), at(0), group_spec,
            by_part(row_count), by_part(HALO), by_part(short_taps),
        ],
        out_specs=[by_part(row_count), by_part(HALO), by_part(HALO), by_part(HALO), group_spec],
        out_shape=[
            jax.ShapeDtypeStruct((row_count, 3 * channels), BF),
            jax.ShapeDtypeStruct((HALO, 3 * channels), F32),
            jax.ShapeDtypeStruct((HALO, 3 * channels), F32),
            jax.ShapeDtypeStruct((HALO, 3 * channels), F32),
            jax.ShapeDtypeStruct((group_count, tap_count), F32),
        ],
        scratch_shapes=[
            pltpu.VMEM((per * tap_count, 2 * tap_count), BF),
            pltpu.VMEM((2 * tap_count, LANES), BF),
            pltpu.VMEM((per * row_count, LANES), BF),
            pltpu.VMEM((3, row_count + HALO, width), F32),
            pltpu.VMEM((row_count + HALO, LANES), F32),
        ],
        compiler_params=pltpu.CompilerParams(vmem_limit_bytes=limit),
        cost_estimate=pl.CostEstimate(
            flops=8 * per * tap_count * row_count * channels,
            bytes_accessed=40 * row_count * channels, transcendentals=0,
        ),
    )(
        grad_gated, grad_next, features, features, features, mixed, mixer_in, lead, filt,
        tokens, rim, short_filter,
    )

    follow = shifted(head.astype(BF), "seq", -1).astype(F32)
    beyond = jnp.concatenate([jnp.zeros_like(follow), follow], axis=0)
    for j in range(short_taps):
        tail = tail + short_filter[j] * beyond[j : j + HALO]
    grad_tokens = lax.dynamic_update_slice(grad_tokens, tail.astype(BF), (row_count - HALO, 0))

    summed = all_reduce_small(
        jnp.concatenate([short_local.reshape(-1), long_local.reshape(-1)])
    )
    cut = HALO * 3 * channels
    grad_short = summed[:cut].reshape(HALO, 3 * channels)[:short_taps]
    grad_long = summed[cut:].reshape(group_count, tap_count)[:, ::-1]
    return (output[None], grad_tokens[None], grad_short, grad_long, grad_weight)


def solution(mesh):
    return jax.shard_map(
        shards,
        mesh=mesh,
        in_specs=(P("dp", "seq", None), P(), P(), P("dp", "seq"), P("dp", None, "seq")),
        out_specs=(P("dp", None, "seq"), P("dp", "seq", None), P(), P(), P("dp", "seq")),
        check_vma=False,
    )
```

time: 869 us -> 339 us (0.39)
  local copies, waits for them, and re-layouts: 417 us -> 16.4 us
  waiting for transfers between devices: 277 us -> 165 us
  Pallas kernels: 0 us -> 91.5 us
  other arithmetic: 63.3 us -> 13.1 us
  matrix products: 71.3 us -> 26.9 us
  starting transfers between devices: 20.9 us -> 11.7 us
    gather x4 -> x0, local copies, waits for them, and re-layouts: 305 us -> none  [tap_table(): taken = jnp.take(filters, clipped, axis=1)]
    psum x1 -> x0, waiting for transfers between devices: 102 us -> none  [shards(): grad_short = lax.psum(short_local, ('dp', 'seq'))]
    pallas_call x0 -> x4, Pallas kernels: none -> 91.5 us  [the longest x1 37.4 us: shards(): pl.pallas_call(functools.partial(backward_kernel, per), grid=(nb, 3), in_...]
    all_gather x1, waiting for transfers between devices: 0.02 us -> 70.5 us  [shards(): all_rows = lax.all_gather(gated, 'seq', axis=0, tiled=True)]
    reshape x4 -> x1, local copies, waits for them, and re-layouts: 69.3 us -> 0.82 us  [shards(): grad_short = summed[:cut].reshape(HALO, 3 * channels)[:short_taps]]
    all_gather x1, waiting for transfers between devices: 57.3 us -> 11.8 us  [shards(): weights = lax.all_gather(out_weight, 'dp', axis=0, tiled=True)]
    dot_general x4 -> x1, matrix products: 52.6 us -> 8.31 us  [shards(): output = jnp.dot(all_rows, weights, preferred_element_type=F32).astype(BF)]
    reduce_scatter x1, waiting for transfers between devices: 43.1 us -> 0.01 us  [shards(): lax.psum_scatter(weight_grad.astype(BF), 'dp', scatter_dimension=0, tiled...]
  transfers between devices with their start and end apart: 9 -> 8, of which waited for: 6 -> 4; matrix products, arithmetic and copies ran while one was open for 57% -> 13% of each run, Pallas kernels for 0% -> 27%
where the time goes in v1:
time: 339 us
  waiting for transfers between devices  165 us (49%)
  Pallas kernels  91.5 us (27%)
  matrix products  26.9 us (8%)
  local copies, waits for them, and re-layouts  16.4 us (5%)
  between operations  14.1 us (4%)
  other arithmetic  13.1 us (4%)
  starting transfers between devices  11.7 us (3%)
    reduce_scatter x1, waiting for transfers between devices, shards(): lax.psum_scatter(lax.dot_general(upstream, weights, (((1,), (1,)), ((), (...  80.7 us
    all_gather x1, waiting for transfers between devices, shards(): all_rows = lax.all_gather(gated, 'seq', axis=0, tiled=True)  70.5 us
    pallas_call x1, Pallas kernels, shards(): pl.pallas_call(functools.partial(backward_kernel, per), grid=(nb, 3), in_...  37.4 us
    pallas_call x1, Pallas kernels, all_reduce_small(): pl.pallas_call(functools.partial(reduce_kernel, n_dp, n_seq), out_shape=j...  34 us
    pallas_call x1, Pallas kernels, shards(): pl.pallas_call(functools.partial(mixed_kernel, per), grid=(nb,), in_specs...  13.3 us
    all_gather x1, waiting for transfers between devices, shards(): weights = lax.all_gather(out_weight, 'dp', axis=0, tiled=True)  11.8 us
    ppermute x4, starting transfers between devices, shifted(): return lax.ppermute(x, axis, pairs)  11.6 us
    unnamed x45, local copies, waits for them, and re-layouts  10.7 us
  transfers between devices with their start and end apart: 8, of which 4 were waited for; matrix products, arithmetic and copies ran while one was open for 13% of the time, Pallas kernels for 27%

profile of v1, /device:TPU:0, one launch (start us, length us, event | category | flops | bytes accessed | tf_op | source)
XLA Modules:
  0.0 338.5 jit_solution(7237887470859925329)
XLA Ops:
  8.0 1.0 slice_bitcast_fusion
  8.9 2.4 collective-permute-start
  11.3 1.0 collective-permute-done
  12.4 1.9 copy-done.3
  14.3 1.0 copy-done.6
  15.3 6.7 %shard_map.92 = (f32[128,12288]{1,0:T(8,128)S(1)}, bf16[128,4096]{1,0:T(8,128)(2,1)S(1)}) custom-call(bf16[128,12288]{1,0:T(8,128)(2,1)S(1)} %bitcast.32, f32[8,12288]{1,0:T(8,128)S(1)} %convert_element_type.31.rim_ref, f32[7,12288]{1,0:T(8,128)S(1)} %copy-done.6), custom_call_target="tpu_custom_call" | custom-call | flops 22020096 | bytes 10485760 | tf_op jit(solution)/shard_map/pallas_call | solution.py:263
  22.0 2.6 copy-done.1
  24.7 6.2 %collective-permute-start.1 = (bf16[128,4096]{1,0:T(8,128)(2,1)S(1)}, bf16[128,4096]{1,0:T(8,128)(2,1)S(1)}, u32[]{:S(2)}, u32[]{:S(2)}) collective-permute-start(bf16[128,4096]{1,0:T(8,128)(2,1)S(1)} %get-tuple-element.14.mix_ref), channel_id=1, source_target_pairs={{0,1},{1,2},{2,3},{3,4},{4,5},{5,6},{6,7},{8,9},{9,10},{10,11},{11... | collective-permute-start | bytes 3145736 | tf_op jit(solution)/shard_map/ppermute | solution.py:19
  30.9 0.7 slice.94
  32.3 1.6 slice.75
  34.0 1.1 pad_maximum_fusion.1.filt_ref
  35.1 2.8 copy-done.2
  37.8 13.3 %shard_map.93 = (f32[128,4096]{1,0:T(8,128)S(1)}, bf16[128,4096]{1,0:T(8,128)(2,1)S(1)}) custom-call(bf16[128,4096]{1,0:T(8,128)(2,1)S(1)} %get-tuple-element.14.mix_ref, bf16[128,4096]{1,0:T(8,128)(2,1)S(1)} %collective-permute-done.1.lead_ref, f32[128,12288]{1,0:T(8,128)S(1)} %copy-done.2, f32[256,128]{1,0:T(8,128)S(1)} %pad_maximum_fusion.1.filt_ref), custom_call_target="tpu_custom_call" | custom-call | flops 2147483648 | bytes 7340032 | tf_op jit(solution)/shard_map/pallas_call | solution.py:284
  51.2 1.3 copy-done.8
  52.5 1.0 copy-done.10
  53.5 11.8 %all-gather.5.cloned.1.call-done = bf16[4096,512]{1,0:T(8,128)(2,1)} async-done(((bf16[1024,512]{1,0:T(8,128)(2,1)}), bf16[4096,512]{1,0:T(8,128)(2,1)}) %all-gather.5.cloned.1.call-update) | async-done | bytes 4194320 | tf_op jit(solution)/shard_map/all_gather | solution.py:256
  65.3 8.9 %convolution_convert_fusion = bf16[1024,4096]{1,0:T(8,128)(2,1)} fusion(bf16[4096,512]{1,0:T(8,128)(2,1)} %all-gather.5.cloned.1.call-done, bf16[1,1024,512]{2,1,0:T(8,128)(2,1)S(1)} %copy-done), kind=kOutput, calls=%fused_computation | convolution fusion | flops 4299161600 | bytes 13631488 | tf_op jit(solution)/shard_map/dot_general | solution.py:306
  74.3 1.5 convert_element_type.32.filt_ref
  75.8 3.3 slice_multiply_fusion.6
  79.1 70.5 %all-gather.3.cloned.1.call-done = bf16[1024,4096]{1,0:T(8,128)(2,1)} async-done(((bf16[128,4096]{1,0:T(8,128)(2,1)}), bf16[1024,4096]{1,0:T(8,128)(2,1)}) %all-gather.3.cloned.1.call-update) | async-done | bytes 8388624 | tf_op jit(solution)/shard_map/all_gather | solution.py:304
  149.6 9.7 %convolution_convert_fusion.1 = bf16[4096,512]{1,0:T(8,128)(2,1)} fusion(bf16[1024,4096]{1,0:T(8,128)(2,1)} %all-gather.3.cloned.1.call-done, bf16[1,1024,512]{2,1,0:T(8,128)(2,1)S(1)} %copy-done), kind=kOutput, calls=%fused_computation.1 | convolution fusion | flops 4297064448 | bytes 13631488 | tf_op jit(solution)/shard_map/dot_general | solution.py:313
  159.3 80.7 %reduce-scatter.3.cloned.1.call-done.gg_ref = bf16[128,4096]{1,0:T(8,128)(2,1)} async-done(((bf16[1024,4096]{1,0:T(8,128)(2,1)}), bf16[128,4096]{1,0:T(8,128)(2,1)}) %reduce-scatter.3.cloned.1.call-update) | async-done | bytes 1048592 | tf_op jit(solution)/shard_map/reduce_scatter | solution.py:305
  240.0 2.2 multiply_convert_fusion
  242.3 1.6 collective-permute-start.2
  243.9 8.3 %fusion = bf16[1,1024,512]{2,1,0:T(8,128)(2,1)} fusion(bf16[1024,4096]{1,0:T(8,128)(2,1)} %all-gather.3.cloned.1.call-done, bf16[4096,512]{1,0:T(8,128)(2,1)S(1)} %copy-done.21), kind=kOutput, calls=%fused_computation.4 | convolution fusion | flops 4295491584 | bytes 13631488 | tf_op jit(solution)/shard_map/dot_general | solution.py:319
  252.2 37.4 %shard_map.94 = (bf16[128,12288]{1,0:T(8,128)(2,1)}, f32[8,12288]{1,0:T(8,128)S(1)}, f32[8,12288]{1,0:T(8,128)S(1)}, f32[8,12288]{1,0:T(8,128)S(1)}, f32[256,128]{1,0:T(8,128)S(1)}) custom-call(bf16[128,4096]{1,0:T(8,128)(2,1)S(1)} %copy-done.5, bf16[128,4096]{1,0:T(8,128)(2,1)S(1)} %collective-permute-done.2.next_ref, f32[128,12288]{1,0:T(8,128)} %copy-done.1, ...), custom_call_target="tpu_custom_call" | custom-call | flops 4294967296 | bytes 20971520 | tf_op jit(solution)/shard_map/pallas_call | solution.py:325
  289.9 1.4 collective-permute-start.3
  291.3 34.0 %shard_map.95 = f32[4,8,32,128]{3,2,1,0:T(8,128)S(1)} custom-call(f32[4,8,32,128]{3,2,1,0:T(8,128)S(1)} %bitcast.34), custom_call_target="tpu_custom_call" | custom-call | flops 131072 | bytes 1048576 | tf_op jit(solution)/shard_map/pallas_call | solution.py:221
  325.4 0.8 reshape.38
  326.2 0.8 rev.4
  327.1 2.0 bitcast_dynamic-update-slice_fusion
  329.2 2.8 convert_element_type.40
  (58 shorter events, 1.9 us)
Async XLA Ops:
  7.2 58.1 %copy-start = (bf16[1,1024,512]{2,1,0:T(8,128)(2,1)S(1)}, bf16[1,1024,512]{2,1,0:T(8,128)(2,1)}, u32[]{:S(2)}) copy-start(bf16[1,1024,512]{2,1,0:T(8,128)(2,1)} %param.9) | copy-start | bytes 3145732
  7.2 58.1 %all-gather.5.cloned.1.call-start = ((), (), s32[]{:S(2)}) async-start(), calls=%async_computation.3 | async-start | bytes 5242880 | tf_op jit(solution)/shard_map/all_gather | solution.py:256
  7.9 141.6 %all-gather.3.cloned.1.call-start = ((), (), s32[]{:S(2)}) async-start(), calls=%async_computation.2 | async-start | bytes 9437184 | tf_op jit(solution)/shard_map/all_gather | solution.py:304
  8.0 23.0 %copy-start.13 = (bf16[256,128]{1,0:T(8,128)(2,1)S(1)}, bf16[256,128]{1,0:T(8,128)(2,1)}, u32[]{:S(2)}) copy-start(bf16[256,128]{1,0:T(8,128)(2,1)} %param.7) | copy-start | bytes 196612
  8.9 3.4 %collective-permute-start = (bf16[8,12288]{1,0:T(8,128)(2,1)S(1)}, bf16[8,12288]{1,0:T(8,128)(2,1)S(1)}, u32[]{:S(2)}, u32[]{:S(2)}) collective-permute-start(bf16[8,12288]{1,0:T(8,128)(2,1)S(1)} %slice_bitcast_fusion), channel_id=1, source_target_pairs={{0,1},{1,2},{2,3},{3,4},{4,5},{5,6},{6,7},{8,9},{9,10},{10,11},{11... | collective-permute-start | bytes 589832 | tf_op jit(solution)/shard_map/ppermute | solution.py:19
  12.4 1.9 copy-start.3
  14.3 1.0 copy-start.6
  22.0 2.6 copy-start.1
  24.7 10.4 %collective-permute-start.1 = (bf16[128,4096]{1,0:T(8,128)(2,1)S(1)}, bf16[128,4096]{1,0:T(8,128)(2,1)S(1)}, u32[]{:S(2)}, u32[]{:S(2)}) collective-permute-start(bf16[128,4096]{1,0:T(8,128)(2,1)S(1)} %get-tuple-element.14.mix_ref), channel_id=1, source_target_pairs={{0,1},{1,2},{2,3},{3,4},{4,5},{5,6},{6,7},{8,9},{9,10},{10,11},{11... | collective-permute-start | bytes 3145736 | tf_op jit(solution)/shard_map/ppermute | solution.py:19
  35.1 2.8 copy-start.2
  51.2 1.3 copy-start.8
  52.5 1.0 copy-start.10
  53.5 186.6 %reduce-scatter.3.cloned.1.call-start = ((), (), s32[]{:S(2)}) async-start(), calls=%async_computation.4 | async-start | bytes 9437184 | tf_op jit(solution)/shard_map/reduce_scatter | solution.py:305
  74.2 255.0 %reduce-scatter.5.cloned.1.call-start = ((), (), s32[]{:S(2)}) async-start(), calls=%async_computation.5 | async-start | bytes 5242880 | tf_op jit(solution)/shard_map/reduce_scatter | solution.py:316
  240.0 3.8 %copy-start.21 = (bf16[4096,512]{1,0:T(8,128)(2,1)S(1)}, bf16[4096,512]{1,0:T(8,128)(2,1)}, u32[]{:S(2)}) copy-start(bf16[4096,512]{1,0:T(8,128)(2,1)} %all-gather.5.cloned.1.call-done) | copy-start | bytes 12582916
  242.3 10.0 %copy-start.4 = (bf16[1,128,12288]{2,1,0:T(8,128)(2,1)S(1)}, bf16[1,128,12288]{2,1,0:T(8,128)(2,1)}, u32[]{:S(2)}) copy-start(bf16[1,128,12288]{2,1,0:T(8,128)(2,1)} %param.5) | copy-start | bytes 9437188
  242.3 9.9 %copy-start.5 = (bf16[128,4096]{1,0:T(8,128)(2,1)S(1)}, bf16[128,4096]{1,0:T(8,128)(2,1)}, u32[]{:S(2)}) copy-start(bf16[128,4096]{1,0:T(8,128)(2,1)} %reduce-scatter.3.cloned.1.call-done.gg_ref) | copy-start | bytes 3145732
  242.3 9.9 %copy-start.7 = (f32[7,12288]{1,0:T(8,128)S(1)}, f32[7,12288]{1,0:T(8,128)}, u32[]{:S(2)}) copy-start(f32[7,12288]{1,0:T(8,128)} %w_ref.3) | copy-start | bytes 1032196
  242.3 9.9 %copy-start.9 = (f32[128,4096]{1,0:T(8,128)S(1)}, f32[128,4096]{1,0:T(8,128)}, u32[]{:S(2)}) copy-start(f32[128,4096]{1,0:T(8,128)} %copy-done.8) | copy-start | bytes 6291460
  242.3 9.9 %copy-start.11 = (f32[256,128]{1,0:T(8,128)S(1)}, f32[256,128]{1,0:T(8,128)}, u32[]{:S(2)}) copy-start(f32[256,128]{1,0:T(8,128)} %convert_element_type.32.filt_ref) | copy-start | bytes 393220
  242.3 9.9 %collective-permute-start.2 = (bf16[128,4096]{1,0:T(8,128)(2,1)S(1)}, bf16[128,4096]{1,0:T(8,128)(2,1)S(1)}, u32[]{:S(2)}, u32[]{:S(2)}) collective-permute-start(bf16[128,4096]{1,0:T(8,128)(2,1)S(1)} %multiply_convert_fusion), channel_id=1, source_target_pairs={{1,0},{2,1},{3,2},{4,3},{5,4},{6,5},{7,6},{9,8},{10,9},{11,10},{12... | collective-permute-start | bytes 3145736 | tf_op jit(solution)/shard_map/ppermute | solution.py:19
  289.7 35.6 %copy-start.12 = (f32[8,12288]{1,0:T(8,128)}, f32[8,12288]{1,0:T(8,128)S(1)}, u32[]{:S(2)}) copy-start(f32[8,12288]{1,0:T(8,128)S(1)} %get-tuple-element.19) | copy-start | bytes 1179652
  289.7 37.4 %copy-start.14 = (f32[1,12288]{1,0:T(1,128)S(1)}, f32[1,12288]{1,0:T(1,128)}, u32[]{:S(2)}) copy-start(f32[1,12288]{1,0:T(1,128)} %get-tuple-element.23) | copy-start | bytes 147460
  289.7 37.4 %copy-start.15 = (f32[1,12288]{1,0:T(1,128)S(1)}, f32[1,12288]{1,0:T(1,128)}, u32[]{:S(2)}) copy-start(f32[1,12288]{1,0:T(1,128)} %get-tuple-element.24) | copy-start | bytes 147460
  289.7 37.4 %copy-start.16 = (f32[1,12288]{1,0:T(1,128)S(1)}, f32[1,12288]{1,0:T(1,128)}, u32[]{:S(2)}) copy-start(f32[1,12288]{1,0:T(1,128)} %get-tuple-element.25) | copy-start | bytes 147460
  289.7 37.4 %copy-start.17 = (f32[1,12288]{1,0:T(1,128)S(1)}, f32[1,12288]{1,0:T(1,128)}, u32[]{:S(2)}) copy-start(f32[1,12288]{1,0:T(1,128)} %get-tuple-element.26) | copy-start | bytes 147460
  289.7 37.4 %copy-start.18 = (f32[1,12288]{1,0:T(1,128)S(1)}, f32[1,12288]{1,0:T(1,128)}, u32[]{:S(2)}) copy-start(f32[1,12288]{1,0:T(1,128)} %get-tuple-element.27) | copy-start | bytes 147460
  289.7 37.4 %copy-start.19 = (f32[1,12288]{1,0:T(1,128)S(1)}, f32[1,12288]{1,0:T(1,128)}, u32[]{:S(2)}) copy-start(f32[1,12288]{1,0:T(1,128)} %get-tuple-element.28) | copy-start | bytes 147460
  289.7 37.4 %copy-start.20 = (f32[1,12288]{1,0:T(1,128)S(1)}, f32[1,12288]{1,0:T(1,128)}, u32[]{:S(2)}) copy-start(f32[1,12288]{1,0:T(1,128)} %get-tuple-element.29) | copy-start | bytes 147460
  289.9 37.2 %collective-permute-start.3 = (bf16[8,12288]{1,0:T(8,128)(2,1)S(1)}, bf16[8,12288]{1,0:T(8,128)(2,1)S(1)}, u32[]{:S(2)}, u32[]{:S(2)}) collective-permute-start(bf16[8,12288]{1,0:T(8,128)(2,1)S(1)} %convert_element_type.37), channel_id=1, source_target_pairs={{1,0},{2,1},{3,2},{4,3},{5,4},{6,5},{7,6},{9,8},{10,9},{11,10},{12... | collective-permute-start | bytes 589832 | tf_op jit(solution)/shard_map/ppermute | solution.py:19
Sparse Core Ops, SparseCore 0:
  9.9 55.3 all-gather.4
  67.5 82.0 all-gather.2
  151.9 88.1 reduce-scatter.2
  242.9 51.0 reduce-scatter.4

commit v2 on v1

--- a/solution.py
+++ b/solution.py
@@ -108,7 +108,7 @@
 
         def lane_block(b, carry):
             sl = pl.ds(pl.multiple_of(b * LANES, LANES), LANES)
-            gg = gg_ref[:, sl].astype(F32)
+            gg = gg_ref[:, sl]
             gm = (gg * query_ref[:, sl]).astype(BF)
             group_tables(filt_ref, b, per, table, True)
             win[0:rows, :] = gm
@@ -210,6 +210,148 @@
     y_ref[...] = full[...]
 
 
+def line_kernel(n_seq, p_ref, out_ref, own, pair, from_left, from_right,
+                load_sem, pair_send, pair_recv, right_send, right_recv, left_send, left_recv):
+    dp = lax.axis_index("dp")
+    seq = lax.axis_index("seq")
+    chips = n_seq // 2
+    chip, core = lax.div(seq, 2), lax.rem(seq, 2)
+    pieces = right_send.shape[1]
+    rows = own.shape[1] // pieces
+    mesh_id = pl.DeviceIdType.MESH
+    ahead = 2
+
+    def at(other_chip, other_core):
+        return (dp, other_chip * 2 + other_core)
+
+    sibling = at(chip, 1 - core)
+    right = at(lax.rem(chip + 1, chips), core)
+    left = at(lax.rem(chip + chips - 1, chips), core)
+    barrier = pltpu.get_barrier_semaphore()
+    for peer in (sibling, right, left):
+        pl.semaphore_signal(barrier, inc=1, device_id=peer, device_id_type=mesh_id)
+    pl.semaphore_wait(barrier, 3)
+
+    order = []
+    for s in range(chips):
+        for c in (chips - 1 - s, s):
+            if c not in order:
+                order.append(c)
+    swaps, loads = {}, {}
+    for c in order:
+        swaps[c] = pltpu.make_async_remote_copy(
+            src_ref=p_ref.at[c, 1 - core], dst_ref=pair.at[c], send_sem=pair_send.at[c],
+            recv_sem=pair_recv.at[c], device_id=sibling, device_id_type=mesh_id,
+        )
+        swaps[c].start()
+        loads[c] = pltpu.make_async_copy(p_ref.at[c, core], own.at[c], load_sem.at[c])
+        loads[c].start()
+
+    def piece(k):
+        return pl.ds(k * rows, rows)
+
+    def hop(rightward, c, k):
+        send, recv, dst, peer = (
+            (right_send, right_recv, from_left, right)
+            if rightward
+            else (left_send, left_recv, from_right, left)
+        )
+        return pltpu.make_async_remote_copy(
+            src_ref=own.at[c, piece(k)], dst_ref=dst.at[c, piece(k)], send_sem=send.at[c, k],
+            recv_sem=recv.at[c, k], device_id=peer, device_id_type=mesh_id,
+        )
+
+    steps = [(s, k) for s in range(chips - 1) for k in range(pieces)]
+    ready = set()
+
+    def target(rightward, s):
+        return chips - 1 - s if rightward else s
+
+    def valid(rightward, s):
+        return target(rightward, s) > chip if rightward else target(rightward, s) < chip
+
+    for n, (s, k) in enumerate(steps):
+        for rightward in (True, False):
+            c = target(rightward, s)
+            if c not in ready:
+                ready.add(c)
+                loads[c].wait()
+                swaps[c].wait()
+
+            @pl.when(valid(rightward, s))
+            def _():
+                sl = piece(k)
+                inbox = from_left if rightward else from_right
+                inner = chip > 0 if rightward else chip < chips - 1
+                both = own[c, sl].astype(F32) + pair[c, sl].astype(F32)
+
+                @pl.when(inner)
+                def _():
+                    hop(rightward, c, k).wait_recv()
+                    own[c, sl] = (both + inbox[c, sl].astype(F32)).astype(BF)
+
+                @pl.when(jnp.logical_not(inner))
+                def _():
+                    own[c, sl] = both.astype(BF)
+
+                if n >= ahead:
+                    before, piece_before = steps[n - ahead]
+                    hop(rightward, target(rightward, before), piece_before).wait_send()
+                hop(rightward, c, k).start()
+
+    for c in order:
+        if c not in ready:
+            ready.add(c)
+            loads[c].wait()
+            swaps[c].wait()
+    for c in range(chips):
+
+        @pl.when(chip == c)
+        def _():
+            for k in range(pieces):
+                sl = piece(k)
+                out_ref[sl, :] = own[c, sl].astype(F32) + pair[c, sl].astype(F32)
+                if c > 0:
+                    hop(True, c, k).wait_recv()
+                    out_ref[sl, :] += from_left[c, sl].astype(F32)
+                if c < chips - 1:
+                    hop(False, c, k).wait_recv()
+                    out_ref[sl, :] += from_right[c, sl].astype(F32)
+            for rightward in (True, False):
+                sent = chips - 1 - c if rightward else c
+                count = sent * pieces
+                for n in range(max(0, count - ahead), count):
+                    s, k = steps[n]
+                    hop(rightward, target(rightward, s), k).wait_send()
+
+
+def sum_over_line(partial, row_count):
+    n_seq = lax.axis_size("seq")
+    chips = n_seq // 2
+    channels = partial.shape[1]
+    pieces = max(1, row_count // 32)
+    dma = pltpu.SemaphoreType.DMA
+    slots = pltpu.VMEM((chips, row_count, channels), BF)
+    return pl.pallas_call(
+        functools.partial(line_kernel, n_seq),
+        out_shape=jax.ShapeDtypeStruct((row_count, channels), F32),
+        in_specs=[pl.BlockSpec(memory_space=pl.ANY)],
+        out_specs=pl.BlockSpec(memory_space=pltpu.VMEM),
+        scratch_shapes=[
+            slots, slots, slots, slots,
+            dma((chips,)), dma((chips,)), dma((chips,)),
+            dma((chips, pieces)), dma((chips, pieces)),
+            dma((chips, pieces)), dma((chips, pieces)),
+        ],
+        compiler_params=pltpu.CompilerParams(
+            collective_id=1, has_side_effects=True, vmem_limit_bytes=48 << 20
+        ),
+        cost_estimate=pl.CostEstimate(
+            flops=8 * row_count * channels, bytes_accessed=300_000_000, transcendentals=0
+        ),
+    )(partial.reshape(chips, 2, row_count, channels))
+
+
 def all_reduce_small(flat):
     n_dp, n_seq = lax.axis_size("dp"), lax.axis_size("seq")
     devices = n_dp * n_seq
@@ -302,13 +444,11 @@
     )(mixer_in, lead, features, turned)
 
     all_rows = lax.all_gather(gated, "seq", axis=0, tiled=True)
-    grad_gated = lax.psum_scatter(
+    grad_gated = sum_over_line(
         lax.dot_general(
             upstream, weights, (((1,), (1,)), ((), ())), preferred_element_type=F32
         ).astype(BF),
-        "seq",
-        scatter_dimension=0,
-        tiled=True,
+        row_count,
     )
     weight_grad = lax.dot_general(
         all_rows, upstream, (((0,), (0,)), ((), ())), preferred_element_type=F32
@@ -318,7 +458,7 @@
     ).astype(F32)
     output = jnp.dot(all_rows, weights, preferred_element_type=F32).astype(BF)
 
-    grad_mixed_in = (grad_gated.astype(F32) * features[:, :channels]).astype(BF)
+    grad_mixed_in = (grad_gated * features[:, :channels]).astype(BF)
     grad_next = shifted(grad_mixed_in, "seq", -1)
     at = lambda off: pl.BlockSpec((row_count, width), lambda j, p: (0, off * nb + j))
     group_spec = pl.BlockSpec((groups, tap_count), lambda j, p: (j, 0))

time: 339 us -> 333 us (0.982)
  waiting for transfers between devices: 165 us -> 13.1 us
  Pallas kernels: 91.5 us -> 228 us
  local copies, waits for them, and re-layouts: 16.4 us -> 24.3 us
    pallas_call x0 -> x1, Pallas kernels: none -> 138 us  [sum_over_line(): pl.pallas_call(functools.partial(line_kernel, n_seq), out_shape=jax.Shape...]
    reduce_scatter x1 -> x0, waiting for transfers between devices: 80.7 us -> none  [shards(): lax.psum_scatter(lax.dot_general(upstream, weights, (((1,), (1,)), ((), (...]
    all_gather x1, waiting for transfers between devices: 70.5 us -> 0.02 us  [shards(): all_rows = lax.all_gather(gated, 'seq', axis=0, tiled=True)]
    unnamed x45 -> x49, local copies, waits for them, and re-layouts: 10.7 us -> 18.6 us
  transfers between devices with their start and end apart: 8 -> 7, of which waited for: 4 -> 2; matrix products, arithmetic and copies ran while one was open for 13% -> 13% of each run, Pallas kernels for 27% -> 69%
where the time goes in v2:
time: 333 us; the launch traced here: 332 us
  Pallas kernels  228 us (68%)
  matrix products  26.6 us (8%)
  local copies, waits for them, and re-layouts  24.3 us (7%)
  between operations  14.1 us (4%)
  other arithmetic  13.3 us (4%)
  waiting for transfers between devices  13.1 us (4%)
  starting transfers between devices  11.6 us (3%)
    pallas_call x1, Pallas kernels, sum_over_line(): pl.pallas_call(functools.partial(line_kernel, n_seq), out_shape=jax.Shape...  138 us
    pallas_call x1, Pallas kernels, shards(): pl.pallas_call(functools.partial(backward_kernel, per), grid=(nb, 3), in_...  37.6 us
    pallas_call x1, Pallas kernels, all_reduce_small(): pl.pallas_call(functools.partial(reduce_kernel, n_dp, n_seq), out_shape=j...  33.1 us
    unnamed x49, local copies, waits for them, and re-layouts  18.6 us
    pallas_call x1, Pallas kernels, shards(): pl.pallas_call(functools.partial(mixed_kernel, per), grid=(nb,), in_specs...  13.3 us
    ppermute x4, starting transfers between devices, shifted(): return lax.ppermute(x, axis, pairs)  11.5 us
    all_gather x1, waiting for transfers between devices, shards(): weights = lax.all_gather(out_weight, 'dp', axis=0, tiled=True)  11.4 us
    dot_general x1, matrix products, shards(): lax.dot_general(all_rows, upstream, (((0,), (0,)), ((), ())), preferred_e...  9.75 us
  transfers between devices with their start and end apart: 7, of which 2 were waited for; matrix products, arithmetic and copies ran while one was open for 13% of the time, Pallas kernels for 69%

profile of v2, /device:TPU:0, one launch (start us, length us, event | category | flops | bytes accessed | tf_op | source)
XLA Modules:
  0.0 331.5 jit_solution(18208137500542647635)
XLA Ops:
  8.0 1.0 slice_bitcast_fusion
  8.9 2.4 collective-permute-start
  11.3 1.0 collective-permute-done
  12.4 1.9 copy-done.3
  14.3 1.0 copy-done.9
  15.3 6.7 %shard_map.92 = (f32[128,12288]{1,0:T(8,128)S(1)}, bf16[128,4096]{1,0:T(8,128)(2,1)S(1)}) custom-call(bf16[128,12288]{1,0:T(8,128)(2,1)S(1)} %bitcast.33, f32[8,12288]{1,0:T(8,128)S(1)} %convert_element_type.28.rim_ref, f32[7,12288]{1,0:T(8,128)S(1)} %copy-done.9), custom_call_target="tpu_custom_call" | custom-call | flops 22020096 | bytes 10485760 | tf_op jit(solution)/shard_map/pallas_call | solution.py:405
  22.0 2.6 copy-done.1
  24.7 6.2 %collective-permute-start.1 = (bf16[128,4096]{1,0:T(8,128)(2,1)S(1)}, bf16[128,4096]{1,0:T(8,128)(2,1)S(1)}, u32[]{:S(2)}, u32[]{:S(2)}) collective-permute-start(bf16[128,4096]{1,0:T(8,128)(2,1)S(1)} %get-tuple-element.14.mix_ref), channel_id=1, source_target_pairs={{0,1},{1,2},{2,3},{3,4},{4,5},{5,6},{6,7},{8,9},{9,10},{10,11},{11... | collective-permute-start | bytes 3145736 | tf_op jit(solution)/shard_map/ppermute | solution.py:19
  32.3 1.6 slice.75
  34.0 1.1 pad_maximum_fusion.1.filt_ref
  35.1 3.2 copy-done.2
  38.2 13.3 %shard_map.93 = (f32[128,4096]{1,0:T(8,128)S(1)}, bf16[128,4096]{1,0:T(8,128)(2,1)S(1)}) custom-call(bf16[128,4096]{1,0:T(8,128)(2,1)S(1)} %get-tuple-element.14.mix_ref, bf16[128,4096]{1,0:T(8,128)(2,1)S(1)} %collective-permute-done.1.lead_ref, f32[128,12288]{1,0:T(8,128)S(1)} %copy-done.2, f32[256,128]{1,0:T(8,128)S(1)} %pad_maximum_fusion.1.filt_ref), custom_call_target="tpu_custom_call" | custom-call | flops 2147483648 | bytes 7340032 | tf_op jit(solution)/shard_map/pallas_call | solution.py:426
  51.6 1.3 copy-done.11
  52.9 1.0 copy-done.13
  53.9 11.4 %all-gather.5.cloned.1.call-done = bf16[4096,512]{1,0:T(8,128)(2,1)} async-done(((bf16[1024,512]{1,0:T(8,128)(2,1)}), bf16[4096,512]{1,0:T(8,128)(2,1)}) %all-gather.5.cloned.1.call-update) | async-done | bytes 4194320 | tf_op jit(solution)/shard_map/all_gather | solution.py:398
  65.3 8.9 %convolution_convert_fusion = bf16[1024,4096]{1,0:T(8,128)(2,1)} fusion(bf16[4096,512]{1,0:T(8,128)(2,1)} %all-gather.5.cloned.1.call-done, bf16[1,1024,512]{2,1,0:T(8,128)(2,1)S(1)} %copy-done), kind=kOutput, calls=%fused_computation | convolution fusion | flops 4299161600 | bytes 13631488 | tf_op jit(solution)/shard_map/dot_general | solution.py:448
  74.2 137.7 %shard_map.94.gg_ref = f32[128,4096]{1,0:T(8,128)S(1)} custom-call(bf16[4,2,128,4096]{3,2,1,0:T(8,128)(2,1)} %bitcast.38), custom_call_target="tpu_custom_call" | custom-call | flops 4194304 | bytes 300000000 | tf_op jit(solution)/shard_map/pallas_call | solution.py:335
  211.9 2.8 multiply_convert_fusion
  214.6 1.5 collective-permute-start.2
  216.1 9.7 %convolution_convert_fusion.1 = bf16[4096,512]{1,0:T(8,128)(2,1)} fusion(bf16[1024,4096]{1,0:T(8,128)(2,1)} %all-gather.3.cloned.1.call-done, bf16[1,1024,512]{2,1,0:T(8,128)(2,1)S(1)} %copy-done), kind=kOutput, calls=%fused_computation.1 | convolution fusion | flops 4297064448 | bytes 13631488 | tf_op jit(solution)/shard_map/dot_general | solution.py:453
  225.9 3.5 %slice_multiply_fusion.6 = (f32[1,12288]{1,0:T(1,128)}, f32[1,12288]{1,0:T(1,128)}, f32[1,12288]{1,0:T(1,128)}, f32[1,12288]{1,0:T(1,128)}, f32[1,12288]{1,0:T(1...) fusion(f32[7,12288]{1,0:T(8,128)} %w_ref.3), kind=kLoop, calls=%fused_computation.25 | loop fusion | flops 12288 | bytes 688128 | tf_op jit(solution)/shard_map/mul | solution.py:500
  230.3 1.9 copy-done.4
  232.2 1.2 copy-done.6
  233.4 1.2 copy-done.8
  234.6 1.0 copy-done.10
  235.6 2.2 copy-done.12
  237.8 37.6 %shard_map.95 = (bf16[128,12288]{1,0:T(8,128)(2,1)}, f32[8,12288]{1,0:T(8,128)S(1)}, f32[8,12288]{1,0:T(8,128)S(1)}, f32[8,12288]{1,0:T(8,128)S(1)}, f32[256,128]{1,0:T(8,128)S(1)}) custom-call(f32[128,4096]{1,0:T(8,128)S(1)} %shard_map.94.gg_ref, bf16[128,4096]{1,0:T(8,128)(2,1)} %collective-permute-done.2.next_ref, f32[128,12288]{1,0:T(8,128)} %copy-done.1, ...), custom_call_target="tpu_custom_call" | custom-call | flops 4294967296 | bytes 20971520 | tf_op jit(solution)/shard_map/pallas_call | solution.py:465
  275.5 1.4 collective-permute-start.3
  277.0 33.1 %shard_map.96 = f32[4,8,32,128]{3,2,1,0:T(8,128)S(1)} custom-call(f32[4,8,32,128]{3,2,1,0:T(8,128)S(1)} %bitcast.35), custom_call_target="tpu_custom_call" | custom-call | flops 131072 | bytes 1048576 | tf_op jit(solution)/shard_map/pallas_call | solution.py:363
  312.0 2.2 bitcast_dynamic-update-slice_fusion
  314.1 8.0 %fusion = bf16[1,1024,512]{2,1,0:T(8,128)(2,1)} fusion(bf16[1024,4096]{1,0:T(8,128)(2,1)} %all-gather.3.cloned.1.call-done, bf16[4096,512]{1,0:T(8,128)(2,1)S(1)} %copy-done.23), kind=kOutput, calls=%fused_computation.4 | convolution fusion | flops 4295491584 | bytes 13631488 | tf_op jit(solution)/shard_map/dot_general | solution.py:459
  322.1 2.8 convert_element_type.36
  (60 shorter events, 5.1 us)
Async XLA Ops:
  7.2 58.1 %copy-start = (bf16[1,1024,512]{2,1,0:T(8,128)(2,1)S(1)}, bf16[1,1024,512]{2,1,0:T(8,128)(2,1)}, u32[]{:S(2)}) copy-start(bf16[1,1024,512]{2,1,0:T(8,128)(2,1)} %param.9) | copy-start | bytes 3145732
  7.2 58.1 %all-gather.5.cloned.1.call-start = ((), (), s32[]{:S(2)}) async-start(), calls=%async_computation.2 | async-start | bytes 5242880 | tf_op jit(solution)/shard_map/all_gather | solution.py:398
  7.9 208.2 %all-gather.3.cloned.1.call-start = ((), (), s32[]{:S(2)}) async-start(), calls=%async_computation.1 | async-start | bytes 9437184 | tf_op jit(solution)/shard_map/all_gather | solution.py:446
  8.0 22.9 %copy-start.15 = (bf16[256,128]{1,0:T(8,128)(2,1)S(1)}, bf16[256,128]{1,0:T(8,128)(2,1)}, u32[]{:S(2)}) copy-start(bf16[256,128]{1,0:T(8,128)(2,1)} %param.7) | copy-start | bytes 196612
  8.9 3.4 %collective-permute-start = (bf16[8,12288]{1,0:T(8,128)(2,1)S(1)}, bf16[8,12288]{1,0:T(8,128)(2,1)S(1)}, u32[]{:S(2)}, u32[]{:S(2)}) collective-permute-start(bf16[8,12288]{1,0:T(8,128)(2,1)S(1)} %slice_bitcast_fusion), channel_id=1, source_target_pairs={{0,1},{1,2},{2,3},{3,4},{4,5},{5,6},{6,7},{8,9},{9,10},{10,11},{11... | collective-permute-start | bytes 589832 | tf_op jit(solution)/shard_map/ppermute | solution.py:19
  12.4 1.9 copy-start.3
  14.3 1.0 copy-start.9
  22.0 2.6 copy-start.1
  24.7 26.9 %copy-start.5 = (bf16[128,4096]{1,0:T(8,128)(2,1)}, bf16[128,4096]{1,0:T(8,128)(2,1)S(1)}, u32[]{:S(2)}) copy-start(bf16[128,4096]{1,0:T(8,128)(2,1)S(1)} %get-tuple-element.14.mix_ref) | copy-start | bytes 3145732
  24.7 10.4 %collective-permute-start.1 = (bf16[128,4096]{1,0:T(8,128)(2,1)S(1)}, bf16[128,4096]{1,0:T(8,128)(2,1)S(1)}, u32[]{:S(2)}, u32[]{:S(2)}) collective-permute-start(bf16[128,4096]{1,0:T(8,128)(2,1)S(1)} %get-tuple-element.14.mix_ref), channel_id=1, source_target_pairs={{0,1},{1,2},{2,3},{3,4},{4,5},{5,6},{6,7},{8,9},{9,10},{10,11},{11... | collective-permute-start | bytes 3145736 | tf_op jit(solution)/shard_map/ppermute | solution.py:19
  35.1 16.5 %copy-start.7 = (bf16[128,4096]{1,0:T(8,128)(2,1)}, bf16[128,4096]{1,0:T(8,128)(2,1)S(1)}, u32[]{:S(2)}) copy-start(bf16[128,4096]{1,0:T(8,128)(2,1)S(1)} %collective-permute-done.1.lead_ref) | copy-start | bytes 3145732
  35.1 3.2 copy-start.2
  51.6 1.3 copy-start.11
  52.9 1.0 copy-start.13
  53.9 268.3 %reduce-scatter.2.cloned.1.call-start = ((), (), s32[]{:S(2)}) async-start(), calls=%async_computation.3 | async-start | bytes 5242880 | tf_op jit(solution)/shard_map/reduce_scatter | solution.py:456
  214.6 15.6 %collective-permute-start.2 = (bf16[128,4096]{1,0:T(8,128)(2,1)}, bf16[128,4096]{1,0:T(8,128)(2,1)}, u32[]{:S(2)}, u32[]{:S(2)}) collective-permute-start(bf16[128,4096]{1,0:T(8,128)(2,1)} %multiply_convert_fusion), channel_id=1, source_target_pairs={{1,0},{2,1},{3,2},{4,3},{5,4},{6,5},{7,6},{9,8},{10,9},{11,10},{12... | collective-permute-start | bytes 3145736 | tf_op jit(solution)/shard_map/ppermute | solution.py:19
  230.3 1.9 copy-start.4
  232.1 1.2 copy-start.6
  233.4 1.2 copy-start.8
  234.6 1.0 copy-start.10
  235.6 2.2 copy-start.12
  275.4 34.8 %copy-start.14 = (f32[8,12288]{1,0:T(8,128)}, f32[8,12288]{1,0:T(8,128)S(1)}, u32[]{:S(2)}) copy-start(f32[8,12288]{1,0:T(8,128)S(1)} %get-tuple-element.19) | copy-start | bytes 1179652
  275.4 36.5 %copy-start.16 = (f32[1,12288]{1,0:T(1,128)S(1)}, f32[1,12288]{1,0:T(1,128)}, u32[]{:S(2)}) copy-start(f32[1,12288]{1,0:T(1,128)} %get-tuple-element.23) | copy-start | bytes 147460
  275.4 36.5 %copy-start.17 = (f32[1,12288]{1,0:T(1,128)S(1)}, f32[1,12288]{1,0:T(1,128)}, u32[]{:S(2)}) copy-start(f32[1,12288]{1,0:T(1,128)} %get-tuple-element.24) | copy-start | bytes 147460
  275.4 36.5 %copy-start.18 = (f32[1,12288]{1,0:T(1,128)S(1)}, f32[1,12288]{1,0:T(1,128)}, u32[]{:S(2)}) copy-start(f32[1,12288]{1,0:T(1,128)} %get-tuple-element.25) | copy-start | bytes 147460
  275.4 36.5 %copy-start.19 = (f32[1,12288]{1,0:T(1,128)S(1)}, f32[1,12288]{1,0:T(1,128)}, u32[]{:S(2)}) copy-start(f32[1,12288]{1,0:T(1,128)} %get-tuple-element.26) | copy-start | bytes 147460
  275.4 36.5 %copy-start.20 = (f32[1,12288]{1,0:T(1,128)S(1)}, f32[1,12288]{1,0:T(1,128)}, u32[]{:S(2)}) copy-start(f32[1,12288]{1,0:T(1,128)} %get-tuple-element.27) | copy-start | bytes 147460
  275.4 36.5 %copy-start.21 = (f32[1,12288]{1,0:T(1,128)S(1)}, f32[1,12288]{1,0:T(1,128)}, u32[]{:S(2)}) copy-start(f32[1,12288]{1,0:T(1,128)} %get-tuple-element.28) | copy-start | bytes 147460
  275.4 36.5 %copy-start.22 = (f32[1,12288]{1,0:T(1,128)S(1)}, f32[1,12288]{1,0:T(1,128)}, u32[]{:S(2)}) copy-start(f32[1,12288]{1,0:T(1,128)} %get-tuple-element.29) | copy-start | bytes 147460
  275.5 36.3 %collective-permute-start.3 = (bf16[8,12288]{1,0:T(8,128)(2,1)S(1)}, bf16[8,12288]{1,0:T(8,128)(2,1)S(1)}, u32[]{:S(2)}, u32[]{:S(2)}) collective-permute-start(bf16[8,12288]{1,0:T(8,128)(2,1)S(1)} %convert_element_type.33), channel_id=1, source_target_pairs={{1,0},{2,1},{3,2},{4,3},{5,4},{6,5},{7,6},{9,8},{10,9},{11,10},{12... | collective-permute-start | bytes 589832 | tf_op jit(solution)/shard_map/ppermute | solution.py:19
  311.8 2.3 copy-start.23
Sparse Core Ops, SparseCore 0:
  9.9 55.3 all-gather.4
  67.5 139.1 all-gather.2
  226.0 56.6 reduce-scatter.1

commit v3 on v2

--- a/solution.py
+++ b/solution.py
@@ -210,8 +210,9 @@
     y_ref[...] = full[...]
 
 
-def line_kernel(n_seq, p_ref, out_ref, own, pair, from_left, from_right,
-                load_sem, pair_send, pair_recv, right_send, right_recv, left_send, left_recv):
+def line_kernel(n_seq, p_ref, g_ref, out_ref, all_ref, own, pair, from_left, from_right,
+                load_sem, pair_send, pair_recv, right_send, right_recv, left_send, left_recv,
+                self_sem, line_send, line_recv, near_send, near_recv):
     dp = lax.axis_index("dp")
     seq = lax.axis_index("seq")
     chips = n_seq // 2
@@ -250,6 +251,71 @@
     def piece(k):
         return pl.ds(k * rows, rows)
 
+    keep = pltpu.make_async_copy(g_ref, all_ref.at[chip, core], self_sem)
+    keep.start()
+
+    def source(rightward, s):
+        return chip - s if rightward else chip + s
+
+    def holds(rightward, s):
+        return source(rightward, s) >= 0 if rightward else source(rightward, s) < chips
+
+    def passes(rightward):
+        return chip < chips - 1 if rightward else chip > 0
+
+    def block(rightward, s, k):
+        if s == 0:
+            return g_ref.at[piece(k)]
+        return all_ref.at[source(rightward, s), core, piece(k)]
+
+    def along(rightward, s, k):
+        way = 0 if rightward else 1
+        return pltpu.make_async_remote_copy(
+            src_ref=block(rightward, s, k),
+            dst_ref=all_ref.at[source(rightward, s), core, piece(k)],
+            send_sem=line_send.at[way, s, k], recv_sem=line_recv.at[way, s, k],
+            device_id=right if rightward else left, device_id_type=mesh_id,
+        )
+
+    def across(rightward, s, k):
+        way = 0 if rightward else 1
+        return pltpu.make_async_remote_copy(
+            src_ref=block(rightward, s, k),
+            dst_ref=all_ref.at[source(rightward, s), core, piece(k)],
+            send_sem=near_send.at[way, s, k], recv_sem=near_recv.at[way, s, k],
+            device_id=sibling, device_id_type=mesh_id,
+        )
+
+    def gather_step(s, k):
+        for rightward in (True, False):
+
+            @pl.when(holds(rightward, s))
+            def _():
+                if s > 0:
+                    along(rightward, s - 1, k).wait_recv()
+                if s < chips - 1:
+
+                    @pl.when(passes(rightward))
+                    def _():
+                        along(rightward, s, k).start()
+
+                if s > 0 or rightward:
+                    across(rightward, s, k).start()
+
+    def gather_end(s, k):
+        for rightward in (True, False):
+
+            @pl.when(holds(rightward, s))
+            def _():
+                if s < chips - 1:
+
+                    @pl.when(passes(rightward))
+                    def _():
+                        along(rightward, s, k).wait_send()
+
+                if s > 0 or rightward:
+                    across(rightward, s, k).wait()
+
     def hop(rightward, c, k):
         send, recv, dst, peer = (
             (right_send, right_recv, from_left, right)
@@ -299,6 +365,10 @@
                     hop(rightward, target(rightward, before), piece_before).wait_send()
                 hop(rightward, c, k).start()
 
+        gather_step(s, k)
+
+    for k in range(pieces):
+        gather_step(chips - 1, k)
     for c in order:
         if c not in ready:
             ready.add(c)
@@ -324,24 +394,34 @@
                     s, k = steps[n]
                     hop(rightward, target(rightward, s), k).wait_send()
 
-
-def sum_over_line(partial, row_count):
+    for s in range(chips):
+        for k in range(pieces):
+            gather_end(s, k)
+    keep.wait()
+
+
+def sum_and_gather(partial, gated):
     n_seq = lax.axis_size("seq")
     chips = n_seq // 2
-    channels = partial.shape[1]
+    row_count, channels = gated.shape
     pieces = max(1, row_count // 32)
     dma = pltpu.SemaphoreType.DMA
     slots = pltpu.VMEM((chips, row_count, channels), BF)
     return pl.pallas_call(
         functools.partial(line_kernel, n_seq),
-        out_shape=jax.ShapeDtypeStruct((row_count, channels), F32),
-        in_specs=[pl.BlockSpec(memory_space=pl.ANY)],
-        out_specs=pl.BlockSpec(memory_space=pltpu.VMEM),
+        out_shape=[
+            jax.ShapeDtypeStruct((row_count, channels), F32),
+            jax.ShapeDtypeStruct((chips, 2, row_count, channels), BF),
+        ],
+        in_specs=[pl.BlockSpec(memory_space=pl.ANY)] * 2,
+        out_specs=[pl.BlockSpec(memory_space=pltpu.VMEM), pl.BlockSpec(memory_space=pl.ANY)],
         scratch_shapes=[
             slots, slots, slots, slots,
             dma((chips,)), dma((chips,)), dma((chips,)),
             dma((chips, pieces)), dma((chips, pieces)),
             dma((chips, pieces)), dma((chips, pieces)),
+            dma, dma((2, chips, pieces)), dma((2, chips, pieces)),
+            dma((2, chips, pieces)), dma((2, chips, pieces)),
         ],
         compiler_params=pltpu.CompilerParams(
             collective_id=1, has_side_effects=True, vmem_limit_bytes=48 << 20
@@ -349,7 +429,7 @@
         cost_estimate=pl.CostEstimate(
             flops=8 * row_count * channels, bytes_accessed=300_000_000, transcendentals=0
         ),
-    )(partial.reshape(chips, 2, row_count, channels))
+    )(partial.reshape(chips, 2, row_count, channels), gated)
 
 
 def all_reduce_small(flat):
@@ -443,13 +523,13 @@
         ),
     )(mixer_in, lead, features, turned)
 
-    all_rows = lax.all_gather(gated, "seq", axis=0, tiled=True)
-    grad_gated = sum_over_line(
+    grad_gated, all_rows = sum_and_gather(
         lax.dot_general(
             upstream, weights, (((1,), (1,)), ((), ())), preferred_element_type=F32
         ).astype(BF),
-        row_count,
+        gated,
     )
+    all_rows = all_rows.reshape(-1, channels)
     weight_grad = lax.dot_general(
         all_rows, upstream, (((0,), (0,)), ((), ())), preferred_element_type=F32
     )

time: 333 us -> 312 us (0.937)
  Pallas kernels: 228 us -> 219 us
  local copies, waits for them, and re-layouts: 24.3 us -> 16.8 us
  other arithmetic: 13.3 us -> 9.64 us
    pallas_call x1, Pallas kernels: 138 us -> 128 us  [sum_and_gather(): pl.pallas_call(functools.partial(line_kernel, n_seq), out_shape=[jax.Shap...]
    unnamed x49 -> x55, local copies, waits for them, and re-layouts: 18.6 us -> 11.1 us
  transfers between devices with their start and end apart: 7 -> 6, of which waited for: 2 -> 2; matrix products, arithmetic and copies ran while one was open for 13% -> 7% of each run, Pallas kernels for 69% -> 29%
where the time goes in v3:
time: 312 us; the launch traced here: 311 us
  Pallas kernels  219 us (70%)
  matrix products  28 us (9%)
  local copies, waits for them, and re-layouts  16.8 us (5%)
  between operations  14.5 us (5%)
  starting transfers between devices  11.7 us (4%)
  waiting for transfers between devices  11.5 us (4%)
  other arithmetic  9.64 us (3%)
    pallas_call x1, Pallas kernels, sum_and_gather(): pl.pallas_call(functools.partial(line_kernel, n_seq), out_shape=[jax.Shap...  128 us
    pallas_call x1, Pallas kernels, shards(): pl.pallas_call(functools.partial(backward_kernel, per), grid=(nb, 3), in_...  37.4 us
    pallas_call x1, Pallas kernels, all_reduce_small(): pl.pallas_call(functools.partial(reduce_kernel, n_dp, n_seq), out_shape=j...  33.4 us
    pallas_call x1, Pallas kernels, shards(): pl.pallas_call(functools.partial(mixed_kernel, per), grid=(nb,), in_specs...  13.3 us
    ppermute x4, starting transfers between devices, shifted(): return lax.ppermute(x, axis, pairs)  11.6 us
    unnamed x55, local copies, waits for them, and re-layouts  11.1 us
    all_gather x1, waiting for transfers between devices, shards(): weights = lax.all_gather(out_weight, 'dp', axis=0, tiled=True)  9.76 us
    dot_general x1, matrix products, shards(): lax.dot_general(all_rows, upstream, (((0,), (0,)), ((), ())), preferred_e...  9.75 us
  transfers between devices with their start and end apart: 6, of which 2 were waited for; matrix products, arithmetic and copies ran while one was open for 7% of the time, Pallas kernels for 29%

profile of v3, /device:TPU:0, one launch (start us, length us, event | category | flops | bytes accessed | tf_op | source)
XLA Modules:
  0.0 311.4 jit_solution(14640221585144684716)
XLA Ops:
  7.2 0.7 all-gather.2.cloned.1.call-update
  8.0 1.0 slice_bitcast_fusion
  9.0 2.4 collective-permute-start
  11.4 1.0 collective-permute-done
  12.4 1.9 copy-done.3
  14.3 1.0 copy-done.9
  15.3 6.7 %shard_map.92 = (f32[128,12288]{1,0:T(8,128)S(1)}, bf16[128,4096]{1,0:T(8,128)(2,1)S(1)}) custom-call(bf16[128,12288]{1,0:T(8,128)(2,1)S(1)} %bitcast.34, f32[8,12288]{1,0:T(8,128)S(1)} %convert_element_type.29.rim_ref, f32[7,12288]{1,0:T(8,128)S(1)} %copy-done.9), custom_call_target="tpu_custom_call" | custom-call | flops 22020096 | bytes 10485760 | tf_op jit(solution)/shard_map/pallas_call | solution.py:485
  22.1 2.6 copy-done.1
  24.7 6.2 %collective-permute-start.1 = (bf16[128,4096]{1,0:T(8,128)(2,1)S(1)}, bf16[128,4096]{1,0:T(8,128)(2,1)S(1)}, u32[]{:S(2)}, u32[]{:S(2)}) collective-permute-start(bf16[128,4096]{1,0:T(8,128)(2,1)S(1)} %get-tuple-element.16.mix_ref), channel_id=1, source_target_pairs={{0,1},{1,2},{2,3},{3,4},{4,5},{5,6},{6,7},{8,9},{9,10},{10,11},{11... | collective-permute-start | bytes 3145736 | tf_op jit(solution)/shard_map/ppermute | solution.py:19
  31.0 1.0 slice_multiply_fusion.6
  31.9 0.7 slice.94
  32.7 0.7 slice.93
  34.0 1.6 slice.75
  35.6 1.1 pad_maximum_fusion.1.filt_ref
  36.7 3.2 %copy-done.2 = f32[128,12288]{1,0:T(8,128)S(1)} copy-done((f32[128,12288]{1,0:T(8,128)S(1)}, f32[128,12288]{1,0:T(8,128)}, u32[]{:S(2)}) %copy-start.2) | copy-done | bytes 6291480
  39.9 13.3 %shard_map.93 = (f32[128,4096]{1,0:T(8,128)S(1)}, bf16[128,4096]{1,0:T(8,128)(2,1)S(1)}) custom-call(bf16[128,4096]{1,0:T(8,128)(2,1)S(1)} %get-tuple-element.16.mix_ref, bf16[128,4096]{1,0:T(8,128)(2,1)S(1)} %collective-permute-done.1.lead_ref, f32[128,12288]{1,0:T(8,128)S(1)} %copy-done.2, f32[256,128]{1,0:T(8,128)S(1)} %pad_maximum_fusion.1.filt_ref), custom_call_target="tpu_custom_call" | custom-call | flops 2147483648 | bytes 7340032 | tf_op jit(solution)/shard_map/pallas_call | solution.py:506
  53.3 1.3 copy-done.12
  54.6 1.0 copy-done.14
  55.5 9.8 %all-gather.2.cloned.1.call-done = bf16[4096,512]{1,0:T(8,128)(2,1)} async-done(((bf16[1024,512]{1,0:T(8,128)(2,1)}), bf16[4096,512]{1,0:T(8,128)(2,1)}) %all-gather.2.cloned.1.call-update) | async-done | bytes 4194320 | tf_op jit(solution)/shard_map/all_gather | solution.py:478
  65.3 9.0 %convolution_convert_fusion = bf16[1024,4096]{1,0:T(8,128)(2,1)} fusion(bf16[4096,512]{1,0:T(8,128)(2,1)} %all-gather.2.cloned.1.call-done, bf16[1,1024,512]{2,1,0:T(8,128)(2,1)S(1)} %copy-done), kind=kOutput, calls=%fused_computation | convolution fusion | flops 4299161600 | bytes 13631488 | tf_op jit(solution)/shard_map/dot_general | solution.py:527
  74.3 128.4 %shard_map.94 = (f32[128,4096]{1,0:T(8,128)S(1)}, bf16[4,2,128,4096]{3,2,1,0:T(8,128)(2,1)}) custom-call(bf16[4,2,128,4096]{3,2,1,0:T(8,128)(2,1)} %bitcast.39, bf16[128,4096]{1,0:T(8,128)(2,1)S(1)} %copy-done.15), custom_call_target="tpu_custom_call" | custom-call | flops 4194304 | bytes 300000000 | tf_op jit(solution)/shard_map/pallas_call | solution.py:410
  202.7 9.7 %convolution_convert_fusion.1 = bf16[4096,512]{1,0:T(8,128)(2,1)} fusion(bf16[1024,4096]{1,0:T(8,128)(2,1)} %bitcast.50, bf16[1,1024,512]{2,1,0:T(8,128)(2,1)S(1)} %copy-done), kind=kOutput, calls=%fused_computation.1 | convolution fusion | flops 4297064448 | bytes 13631488 | tf_op jit(solution)/shard_map/dot_general | solution.py:533
  212.5 1.9 multiply_convert_fusion
  214.5 1.6 collective-permute-start.2
  216.1 9.3 %fusion = bf16[1,1024,512]{2,1,0:T(8,128)(2,1)} fusion(bf16[1024,4096]{1,0:T(8,128)(2,1)} %bitcast.51, bf16[4096,512]{1,0:T(8,128)(2,1)S(1)} %copy-done.26), kind=kOutput, calls=%fused_computation.4 | convolution fusion | flops 4295491584 | bytes 13631488 | tf_op jit(solution)/shard_map/dot_general | solution.py:539
  225.4 37.4 %shard_map.95 = (bf16[128,12288]{1,0:T(8,128)(2,1)}, f32[8,12288]{1,0:T(8,128)S(1)}, f32[8,12288]{1,0:T(8,128)S(1)}, f32[8,12288]{1,0:T(8,128)S(1)}, f32[256,128]{1,0:T(8,128)S(1)}) custom-call(f32[128,4096]{1,0:T(8,128)S(1)} %get-tuple-element.20.gg_ref, bf16[128,4096]{1,0:T(8,128)(2,1)S(1)} %collective-permute-done.2.next_ref, f32[128,12288]{1,0:T(8,128)} %copy-done.1, ...), custom_call_target="tpu_custom_call" | custom-call | flops 4294967296 | bytes 20971520 | tf_op jit(solution)/shard_map/pallas_call | solution.py:545
  263.0 1.4 collective-permute-start.3
  264.4 33.4 %shard_map.96 = f32[4,8,32,128]{3,2,1,0:T(8,128)S(1)} custom-call(f32[4,8,32,128]{3,2,1,0:T(8,128)S(1)} %bitcast.36), custom_call_target="tpu_custom_call" | custom-call | flops 131072 | bytes 1048576 | tf_op jit(solution)/shard_map/pallas_call | solution.py:443
  297.9 0.8 reshape.46
  298.7 0.8 rev.4
  299.7 2.0 bitcast_dynamic-update-slice_fusion
  301.7 2.8 convert_element_type.36
  (63 shorter events, 1.1 us)
Async XLA Ops:
  7.2 58.1 %copy-start = (bf16[1,1024,512]{2,1,0:T(8,128)(2,1)S(1)}, bf16[1,1024,512]{2,1,0:T(8,128)(2,1)}, u32[]{:S(2)}) copy-start(bf16[1,1024,512]{2,1,0:T(8,128)(2,1)} %param.9) | copy-start | bytes 3145732
  7.2 58.1 %all-gather.2.cloned.1.call-start = ((), (), s32[]{:S(2)}) async-start(), calls=%async_computation.1 | async-start | bytes 5242880 | tf_op jit(solution)/shard_map/all_gather | solution.py:478
  7.9 293.8 %reduce-scatter.2.cloned.1.call-start = ((), (), s32[]{:S(2)}) async-start(), calls=%async_computation.2 | async-start | bytes 5242880 | tf_op jit(solution)/shard_map/reduce_scatter | solution.py:536
  8.0 23.0 %copy-start.10 = (f32[7,12288]{1,0:T(8,128)S(1)}, f32[7,12288]{1,0:T(8,128)}, u32[]{:S(2)}) copy-start(f32[7,12288]{1,0:T(8,128)} %w_ref.3) | copy-start | bytes 1032196
  8.0 24.0 %copy-start.18 = (bf16[256,128]{1,0:T(8,128)(2,1)S(1)}, bf16[256,128]{1,0:T(8,128)(2,1)}, u32[]{:S(2)}) copy-start(bf16[256,128]{1,0:T(8,128)(2,1)} %param.7) | copy-start | bytes 196612
  9.0 3.4 %collective-permute-start = (bf16[8,12288]{1,0:T(8,128)(2,1)S(1)}, bf16[8,12288]{1,0:T(8,128)(2,1)S(1)}, u32[]{:S(2)}, u32[]{:S(2)}) collective-permute-start(bf16[8,12288]{1,0:T(8,128)(2,1)S(1)} %slice_bitcast_fusion), channel_id=1, source_target_pairs={{0,1},{1,2},{2,3},{3,4},{4,5},{5,6},{6,7},{8,9},{9,10},{10,11},{11... | collective-permute-start | bytes 589832 | tf_op jit(solution)/shard_map/ppermute | solution.py:19
  12.4 1.9 copy-start.3
  14.3 1.0 copy-start.9
  22.1 2.6 copy-start.1
  24.7 28.5 %copy-start.5 = (bf16[128,4096]{1,0:T(8,128)(2,1)}, bf16[128,4096]{1,0:T(8,128)(2,1)S(1)}, u32[]{:S(2)}) copy-start(bf16[128,4096]{1,0:T(8,128)(2,1)S(1)} %get-tuple-element.16.mix_ref) | copy-start | bytes 3145732
  24.7 12.0 %collective-permute-start.1 = (bf16[128,4096]{1,0:T(8,128)(2,1)S(1)}, bf16[128,4096]{1,0:T(8,128)(2,1)S(1)}, u32[]{:S(2)}, u32[]{:S(2)}) collective-permute-start(bf16[128,4096]{1,0:T(8,128)(2,1)S(1)} %get-tuple-element.16.mix_ref), channel_id=1, source_target_pairs={{0,1},{1,2},{2,3},{3,4},{4,5},{5,6},{6,7},{8,9},{9,10},{10,11},{11... | collective-permute-start | bytes 3145736 | tf_op jit(solution)/shard_map/ppermute | solution.py:19
  36.7 16.5 %copy-start.7 = (bf16[128,4096]{1,0:T(8,128)(2,1)}, bf16[128,4096]{1,0:T(8,128)(2,1)S(1)}, u32[]{:S(2)}) copy-start(bf16[128,4096]{1,0:T(8,128)(2,1)S(1)} %collective-permute-done.1.lead_ref) | copy-start | bytes 3145732
  36.7 3.2 %copy-start.2 = (f32[128,12288]{1,0:T(8,128)S(1)}, f32[128,12288]{1,0:T(8,128)}, u32[]{:S(2)}) copy-start(f32[128,12288]{1,0:T(8,128)} %copy-done.1) | copy-start | bytes 18874372
  53.2 1.3 copy-start.12
  65.3 9.0 %copy-start.15 = (bf16[128,4096]{1,0:T(8,128)(2,1)S(1)}, bf16[128,4096]{1,0:T(8,128)(2,1)}, u32[]{:S(2)}) copy-start(bf16[128,4096]{1,0:T(8,128)(2,1)} %copy-done.14) | copy-start | bytes 3145732
  212.5 3.6 %copy-start.26 = (bf16[4096,512]{1,0:T(8,128)(2,1)S(1)}, bf16[4096,512]{1,0:T(8,128)(2,1)}, u32[]{:S(2)}) copy-start(bf16[4096,512]{1,0:T(8,128)(2,1)} %all-gather.2.cloned.1.call-done) | copy-start | bytes 12582916
  214.4 10.9 %copy-start.4 = (bf16[1,128,12288]{2,1,0:T(8,128)(2,1)S(1)}, bf16[1,128,12288]{2,1,0:T(8,128)(2,1)}, u32[]{:S(2)}) copy-start(bf16[1,128,12288]{2,1,0:T(8,128)(2,1)} %param.5) | copy-start | bytes 9437188
  214.4 10.9 %copy-start.6 = (bf16[128,4096]{1,0:T(8,128)(2,1)S(1)}, bf16[128,4096]{1,0:T(8,128)(2,1)}, u32[]{:S(2)}) copy-start(bf16[128,4096]{1,0:T(8,128)(2,1)} %copy-done.5) | copy-start | bytes 3145732
  214.4 10.9 %copy-start.8 = (bf16[128,4096]{1,0:T(8,128)(2,1)S(1)}, bf16[128,4096]{1,0:T(8,128)(2,1)}, u32[]{:S(2)}) copy-start(bf16[128,4096]{1,0:T(8,128)(2,1)} %copy-done.7) | copy-start | bytes 3145732
  214.4 10.9 %copy-start.11 = (f32[7,12288]{1,0:T(8,128)S(1)}, f32[7,12288]{1,0:T(8,128)}, u32[]{:S(2)}) copy-start(f32[7,12288]{1,0:T(8,128)} %w_ref.3) | copy-start | bytes 1032196
  214.5 10.9 %copy-start.13 = (f32[128,4096]{1,0:T(8,128)S(1)}, f32[128,4096]{1,0:T(8,128)}, u32[]{:S(2)}) copy-start(f32[128,4096]{1,0:T(8,128)} %copy-done.12) | copy-start | bytes 6291460
  214.5 10.9 %copy-start.16 = (f32[256,128]{1,0:T(8,128)S(1)}, f32[256,128]{1,0:T(8,128)}, u32[]{:S(2)}) copy-start(f32[256,128]{1,0:T(8,128)} %convert_element_type.30.filt_ref) | copy-start | bytes 393220
  214.5 10.9 %collective-permute-start.2 = (bf16[128,4096]{1,0:T(8,128)(2,1)S(1)}, bf16[128,4096]{1,0:T(8,128)(2,1)S(1)}, u32[]{:S(2)}, u32[]{:S(2)}) collective-permute-start(bf16[128,4096]{1,0:T(8,128)(2,1)S(1)} %multiply_convert_fusion), channel_id=1, source_target_pairs={{1,0},{2,1},{3,2},{4,3},{5,4},{6,5},{7,6},{9,8},{10,9},{11,10},{12... | collective-permute-start | bytes 3145736 | tf_op jit(solution)/shard_map/ppermute | solution.py:19
  262.8 35.1 %copy-start.17 = (f32[8,12288]{1,0:T(8,128)}, f32[8,12288]{1,0:T(8,128)S(1)}, u32[]{:S(2)}) copy-start(f32[8,12288]{1,0:T(8,128)S(1)} %get-tuple-element.23) | copy-start | bytes 1179652
  262.8 36.8 %copy-start.19 = (f32[1,12288]{1,0:T(1,128)S(1)}, f32[1,12288]{1,0:T(1,128)}, u32[]{:S(2)}) copy-start(f32[1,12288]{1,0:T(1,128)} %get-tuple-element.27) | copy-start | bytes 147460
  262.8 36.8 %copy-start.20 = (f32[1,12288]{1,0:T(1,128)S(1)}, f32[1,12288]{1,0:T(1,128)}, u32[]{:S(2)}) copy-start(f32[1,12288]{1,0:T(1,128)} %get-tuple-element.28) | copy-start | bytes 147460
  262.8 36.8 %copy-start.21 = (f32[1,12288]{1,0:T(1,128)S(1)}, f32[1,12288]{1,0:T(1,128)}, u32[]{:S(2)}) copy-start(f32[1,12288]{1,0:T(1,128)} %get-tuple-element.29) | copy-start | bytes 147460
  262.8 36.8 %copy-start.22 = (f32[1,12288]{1,0:T(1,128)S(1)}, f32[1,12288]{1,0:T(1,128)}, u32[]{:S(2)}) copy-start(f32[1,12288]{1,0:T(1,128)} %get-tuple-element.30) | copy-start | bytes 147460
  262.8 36.8 %copy-start.23 = (f32[1,12288]{1,0:T(1,128)S(1)}, f32[1,12288]{1,0:T(1,128)}, u32[]{:S(2)}) copy-start(f32[1,12288]{1,0:T(1,128)} %get-tuple-element.31) | copy-start | bytes 147460
  262.8 36.8 %copy-start.24 = (f32[1,12288]{1,0:T(1,128)S(1)}, f32[1,12288]{1,0:T(1,128)}, u32[]{:S(2)}) copy-start(f32[1,12288]{1,0:T(1,128)} %get-tuple-element.32) | copy-start | bytes 147460
  262.8 36.8 %copy-start.25 = (f32[1,12288]{1,0:T(1,128)S(1)}, f32[1,12288]{1,0:T(1,128)}, u32[]{:S(2)}) copy-start(f32[1,12288]{1,0:T(1,128)} %get-tuple-element.33) | copy-start | bytes 147460
  263.0 36.6 %collective-permute-start.3 = (bf16[8,12288]{1,0:T(8,128)(2,1)S(1)}, bf16[8,12288]{1,0:T(8,128)(2,1)S(1)}, u32[]{:S(2)}, u32[]{:S(2)}) collective-permute-start(bf16[8,12288]{1,0:T(8,128)(2,1)S(1)} %convert_element_type.33), channel_id=1, source_target_pairs={{1,0},{2,1},{3,2},{4,3},{5,4},{6,5},{7,6},{9,8},{10,9},{11,10},{12... | collective-permute-start | bytes 589832 | tf_op jit(solution)/shard_map/ppermute | solution.py:19
  (1 other events, 1.0 us)
Sparse Core Ops, SparseCore 0:
  9.9 55.3 all-gather.1
  212.6 50.9 reduce-scatter.1
